TPU v7x, 32 devices: a whole 2x2x4 slice. The times are simulated.
32 devices in a mesh: dp: 8 (over z, y), rep: 4 (over x, core).
Axes of the slice: x: 2, y: 2, z: 4, core: 2. Of those that a mesh axis runs over, the one named last changes fastest.
Arguments:
- tokens: bfloat16 [1024, 2048], P('dp'), may hold values from -6 to 6
- cotangent: bfloat16 [1024, 2048], P('dp'), may hold values from -6 to 6
- probe_seed: int32 [1024], P('dp'), may hold values from 0 to 1073741823
- w_in: bfloat16 [2048, 8192], P('dp', 'rep'), may hold values from -0.125 to 0.125
- bias: float32 [8192], P('rep'), may hold values from -1.5 to 1.5
- w_out: bfloat16 [8192, 2048], P(('rep', 'dp')), may hold values from -0.0625 to 0.0625
- left_in: bfloat16 [2048], replicated, may hold values from -6 to 6
- left_out: bfloat16 [8192], P('rep'), may hold values from -6 to 6
Outputs:
- output: bfloat16 [1024, 2048], P('dp')
- logdet: float32 [1024], P('dp')
- grad_tokens: float32 [1024, 2048], P('dp')
- grad_in: float32 [2048, 8192], P('dp', 'rep')
- grad_out: float32 [8192, 2048], P(('rep', 'dp'))
All inputs are finite; a program needn't handle non-finite values.
Results may differ from a plain program's by a relative error of at most 0.012.
Values may be sent and summed in bfloat16 or wider, within the bound.
No kernel may reach another device: no remote copies, remote signals or barrier semaphores. Data moves between devices by JAX's collectives and lax.ppermute only.
A program may use at most 128 MiB of HBM per device.

v0:
```python
import jax
import jax.numpy as jnp
from jax import lax
from jax.sharding import Mesh
from jax.sharding import PartitionSpec as P

F32 = jnp.float32
BF16 = jnp.bfloat16
EVERY = ("z", "y", "x", "c")
SWAP = [(0, 1), (1, 0)]


def probe_signs(seeds, width):
    columns = jnp.arange(width, dtype=jnp.int32)
    mixed = seeds[:, None] * 747796405 + columns[None, :] * 1640531527
    mixed = mixed ^ lax.shift_right_logical(mixed, jnp.full_like(mixed, 16))
    mixed = mixed * 668265261
    mixed = mixed ^ lax.shift_right_logical(mixed, jnp.full_like(mixed, 15))
    lowbit = jnp.bitwise_and(lax.shift_right_logical(mixed, jnp.full_like(mixed, 7)), 1)
    return (1 - 2 * lowbit).astype(F32).astype(BF16)


def times(left, right):
    return jnp.dot(left, right, preferred_element_type=F32)


def contract_rows(left, right):
    return lax.dot_general(left, right, (((0,), (0,)), ((), ())), preferred_element_type=F32)


def contract_cols(left, right):
    return lax.dot_general(left, right, (((1,), (1,)), ((), ())), preferred_element_type=F32)


def in_order(own, other, index):
    first = jnp.where(index == 0, own, other)
    second = jnp.where(index == 0, other, own)
    return jnp.concatenate([first, second], 0)


def sum_over(values, names):
    for name in names:
        size, step = lax.axis_size(name), 1
        while step < size:
            pairs = [(place, place ^ step) for place in range(size)]
            values = values + lax.ppermute(values, name, pairs)
            step *= 2
    return values


def spread(block):
    half = block.shape[0] // 2
    x_low = lax.ppermute(block[half:], "x", SWAP)
    y_top = lax.ppermute(block[:half], "y", SWAP)
    x_top = lax.ppermute(block[:half], "x", SWAP)
    y_low = lax.ppermute(block[half:], "y", SWAP)
    far_top = lax.ppermute(y_top, "x", SWAP)
    far_low = lax.ppermute(x_low, "y", SWAP)
    stack = lambda top, low: jnp.concatenate([top, low], 0)
    return stack(x_top, x_low), stack(y_top, y_low), stack(far_top, far_low)


def exchange(to_x, to_y, across):
    return (
        lax.ppermute(to_x, "x", SWAP),
        lax.ppermute(to_y, "y", SWAP),
        lax.ppermute(across, ("y", "x"), [(place, 3 - place) for place in range(4)]),
    )


def fold_cores(part):
    half = part.shape[0] // 2
    got = lax.ppermute(part[half:].astype(BF16), "c", SWAP)
    return (part[:half] + got.astype(F32)).astype(BF16)


def sum_planes(rows):
    got = lax.all_to_all(rows, "z", 0, 0, tiled=True)
    planes = lax.axis_size("z")
    return jnp.sum(got.reshape(planes, rows.shape[0] // planes, -1).astype(F32), 0)


def with_other_core(half):
    return jnp.concatenate([half, lax.ppermute(half, "c", SWAP)], 0)


def gather_rows(quarter):
    return with_other_core(lax.all_gather(quarter, "z", axis=0, tiled=True))


def exchange_shared(to_x, to_y, across):
    half = to_x.shape[0] // 2
    parts = exchange(to_x[:half], to_y[:half], across[:half])
    return tuple(with_other_core(part) for part in parts)


def behind(values, *before):
    return lax.optimization_barrier((values, before))[0]


def on_device(tokens, cotangent, probe_seed, w_in, bias, w_out, left_in, left_out):
    coef = 0.9
    planes = lax.axis_size("z")
    at_z, at_y, at_x, core = (lax.axis_index(name) for name in EVERY)
    count, width = tokens.shape
    rows_in, hid_rep = w_in.shape
    rows_out = w_out.shape[0]
    piece = hid_rep // planes
    quarter = count // 4
    at_dp = at_z * 2 + at_y
    at_rep = at_x * 2 + core

    def own_quarter(array):
        return lax.dynamic_slice_in_dim(array, at_rep * quarter, quarter, 0)

    def rows_of(array, y_index):
        starts = [(2 * plane + y_index) * rows_in for plane in range(planes)]
        return jnp.concatenate(
            [lax.dynamic_slice_in_dim(array, start, rows_in, 1) for start in starts], 1
        )

    def units_of(array, y_index, x_other):
        start = (2 * x_other + y_index) * rows_out
        return lax.dynamic_slice_in_dim(array, start, rows_out, 1)

    in_z = lax.all_to_all(w_in, "z", 1, 0, tiled=True)
    out_x, out_y, out_d = spread(w_out)
    full_out = jnp.concatenate([in_order(w_out, out_y, at_y), in_order(out_x, out_d, at_y)], 0)

    def join_rows(own, other):
        first = jnp.where(at_y == 0, own, other).reshape(planes, 1, rows_in, piece)
        second = jnp.where(at_y == 0, other, own).reshape(planes, 1, rows_in, piece)
        return jnp.concatenate([first, second], 1).reshape(width, piece)

    in_x, in_y, in_d = spread(in_z)
    full_in = jnp.concatenate([join_rows(in_z, in_y), join_rows(in_x, in_d)], 1)

    tok_own = own_quarter(tokens)
    pair = behind(jnp.stack([tok_own, own_quarter(cotangent)]), in_z)
    pair = lax.all_gather(pair, "z", axis=1)
    tok = with_other_core(pair[0].reshape(-1, width))
    cot = with_other_core(pair[1].reshape(-1, width))
    n = tok.shape[0]
    seeds = jnp.where(
        jnp.arange(planes)[:, None] == at_z, own_quarter(probe_seed)[None, :], 0
    ).reshape(-1)
    seeds = with_other_core(sum_over(seeds, ("z",)))
    probe = probe_signs(seeds, width)
    bias_own = lax.dynamic_slice_in_dim(bias, at_z * piece, piece, 0)
    bias_all = jnp.concatenate([bias_own, lax.ppermute(bias_own, "x", SWAP)])

    left_one = left_in.astype(F32)
    slice_one = lax.dynamic_slice_in_dim(left_in, at_dp * rows_in, rows_in, 0)
    slice_two = lax.dynamic_slice_in_dim(left_out, at_dp * rows_out, rows_out, 0)
    p_part = times(slice_one, w_in)
    q_part = times(slice_two, w_out)
    slice_one = slice_one.astype(F32)
    slice_two = slice_two.astype(F32)
    sums = sum_over(
        jnp.concatenate([p_part, q_part, jnp.sum(slice_two * slice_two)[None]]), ("z", "y")
    )
    p_vec = sums[:hid_rep]
    sums = sum_over(jnp.concatenate([sums[hid_rep:], jnp.sum(p_vec * p_vec)[None]]), ("c", "x"))
    q_vec = sums[:width]
    p_norm = sums[-1]
    q_norm = jnp.sum(q_vec * q_vec)
    scale_in = coef * jnp.sqrt(jnp.sum(left_one * left_one) / p_norm)
    scale_out = coef * jnp.sqrt(sums[-2] / q_norm)

    raw = times(jnp.concatenate([tok, probe], 0), full_in)
    raw_z = raw[:n]
    e_one = scale_in * raw[n:]
    tanh_z = jnp.tanh(scale_in * raw_z + bias_all)
    deriv = 1.0 - tanh_z * tanh_z
    act = tanh_z.astype(BF16)
    r_one = (e_one * deriv).astype(BF16)
    j_pair = fold_cores(scale_out * times(r_one, full_out))
    j_one = gather_rows(sum_planes(j_pair).astype(BF16))

    factors = n <= 4 * rows_out
    tok_late, cot_late, seeds_late, probe_late = behind((tok, cot, seeds, probe), j_pair)
    if factors:
        tok_rows = exchange_shared(
            rows_of(tok_late, at_y), rows_of(tok_late, 1 - at_y), rows_of(tok_late, 1 - at_y)
        )
        cot_rows = exchange_shared(cot_late, cot_late, cot_late)
    backs = contract_cols(jnp.concatenate([probe_late, cot_late], 0), full_out)
    raw_b = backs[:n]
    raw_c = backs[n:]
    hd = deriv * (scale_out * raw_b)
    h_round = hd.astype(BF16)

    e_two = scale_in * times(j_one, full_in)
    r_two = (e_two * deriv).astype(BF16)
    j_pair = fold_cores(scale_out * times(r_two, full_out))
    j_two = gather_rows(sum_planes(j_pair).astype(BF16))

    act_late, h_late, seeds_late, probe_late = behind(
        (act, h_round, seeds_late, probe_late), j_pair
    )
    branch = fold_cores(scale_out * times(act_late, full_out))

    def exchange_units(array):
        return exchange(
            units_of(array, at_y, 1), units_of(array, 1 - at_y, 0), units_of(array, 1 - at_y, 1)
        )

    def exchange_pieces(array):
        return exchange(array[:, piece:], array[:, :piece], array[:, piece:])

    if factors:
        h_cols = exchange_pieces(h_late)
        act_units = exchange_units(act_late)
        seeds_x = lax.ppermute(seeds_late, "x", SWAP)
        seeds_y = lax.ppermute(seeds_late, "y", SWAP)
        seeds_d = lax.ppermute(seeds_x, "y", SWAP)
        grad_two = contract_rows(units_of(act_late, at_y, 0), cot)
        for left, right in zip(act_units, cot_rows):
            grad_two = grad_two + contract_rows(left, right)

    w_vec = (probe.astype(F32) - j_one.astype(F32) + j_two.astype(F32)).astype(BF16)
    if factors:
        w_rows = exchange_shared(
            rows_of(w_vec, at_y), rows_of(w_vec, 1 - at_y), rows_of(w_vec, 1 - at_y)
        )
    e_three = scale_in * times(j_two, full_in)
    a_vec = e_one - e_two + e_three
    second = -2.0 * tanh_z * deriv
    dz_vec = scale_out * raw_c * deriv - a_vec * (scale_out * raw_b) * second
    dz_round = dz_vec.astype(BF16)
    g_round = (a_vec * deriv).astype(BF16)

    def block_one(y_index, columns):
        grad = contract_rows(rows_of(tok, y_index), dz_round[:, columns])
        return grad - contract_rows(rows_of(w_vec, y_index), h_round[:, columns])

    own_cols, other_cols = slice(0, piece), slice(piece, 2 * piece)
    if factors:
        dz_cols = exchange_pieces(dz_round)
        started = dz_cols[1]
        grad_one = block_one(at_y, own_cols)
        for left, right in zip(w_rows, h_cols):
            grad_one = grad_one - contract_rows(left, right)
        for left, right in zip(tok_rows, dz_cols):
            grad_one = grad_one + contract_rows(left, right)
    else:
        parts = exchange(
            block_one(at_y, other_cols).astype(BF16),
            block_one(1 - at_y, own_cols).astype(BF16),
            block_one(1 - at_y, other_cols).astype(BF16),
        )
        started = parts[1]
        grad_one = block_one(at_y, own_cols) + sum(part.astype(F32) for part in parts)
    block = grad_one.astype(BF16)
    grad_one = lax.all_to_all(block, "z", 0, 1, tiled=True).astype(F32)

    g_late, a_late, e_late = behind((g_round, a_vec, e_three), started)
    if factors:
        g_units = exchange_units(g_late)
        grad_two = grad_two - contract_rows(units_of(g_late, at_y, 0), probe)
        for left, near in zip(g_units, (seeds_x, seeds_y, seeds_d)):
            grad_two = grad_two - contract_rows(left, probe_signs(near, width))
    else:

        def block_two(y_index, x_other):
            grad = contract_rows(units_of(act, y_index, x_other), cot)
            return grad - contract_rows(units_of(g_late, y_index, x_other), probe)

        parts = exchange(
            block_two(at_y, 1).astype(BF16),
            block_two(1 - at_y, 0).astype(BF16),
            block_two(1 - at_y, 1).astype(BF16),
        )
        grad_two = block_two(at_y, 0) + sum(part.astype(F32) for part in parts)

    dx = sum_planes(fold_cores(scale_in * contract_cols(dz_round, full_in))).astype(BF16)
    branch = sum_planes(behind(branch, j_two))
    output = (tok_own.astype(F32) + branch).astype(BF16)
    output, dx = behind((output, dx), block)
    output = lax.all_gather(output, ("x", "c"), axis=0, tiled=True)
    dx = lax.all_gather(dx, ("x", "c"), axis=0, tiled=True)
    grad_tokens = cotangent.astype(F32) + dx.astype(F32)

    terms = jnp.sum((e_one - e_two / 2.0 + e_late / 3.0) * hd, axis=1)
    inner_one = jnp.sum(dz_round.astype(F32) * raw_z - h_round.astype(F32) * (a_late / scale_in))
    inner_two = jnp.sum(act.astype(F32) * raw_c - g_late.astype(F32) * raw_b)
    inner = jnp.stack([inner_one, inner_two])
    tail = jnp.concatenate([terms, inner])
    got = lax.ppermute(tail, "c", SWAP)
    terms = terms + jnp.concatenate([got[n // 2 : n], got[: n // 2]])
    tail = sum_over(jnp.concatenate([terms, inner + got[n:]]), ("z",))
    terms = lax.dynamic_index_in_dim(tail[:n].reshape(2, planes, quarter), at_z, 1, keepdims=False)
    terms = in_order(terms[0], terms[1], core)
    tail = jnp.concatenate([tail[n:], terms])
    tail_x = lax.ppermute(tail, "x", SWAP)
    logdet = in_order(tail[2:], tail_x[2:], at_x)
    inner = sum_over(tail[:2] + tail_x[:2], ("y",))

    grad_in = scale_in * (grad_one - inner[0] * slice_one[:, None] * p_vec[None, :] / p_norm)
    grad_out = scale_out * (grad_two - inner[1] * slice_two[:, None] * q_vec[None, :] / q_norm)
    return (output, logdet, grad_tokens, grad_in, grad_out)


def solution(mesh):
    fine = Mesh(
        mesh.devices.reshape(mesh.shape["dp"] // 2, 2, mesh.shape["rep"] // 2, 2), EVERY
    )
    dp, rep = ("z", "y"), ("x", "c")
    placed = (
        P(dp, None),
        P(dp, None),
        P(dp),
        P(dp, rep),
        P(rep),
        P(rep + dp, None),
        P(),
        P(rep),
    )
    return jax.shard_map(
        on_device,
        mesh=fine,
        in_specs=placed,
        out_specs=(P(dp, None), P(dp), P(dp, None), P(dp, rep), P(rep + dp, None)),
        check_vma=False,
    )
```

profile of v0, /device:TPU:0, one launch (start us, length us, event | category | flops | bytes accessed | tf_op | source)
XLA Modules:
  0.0 446.8 jit_solution(14036754868742040882)
XLA Ops:
  19.0 4.0 all-to-all-start
  31.7 24.7 %collective-permute-done = f32[4097]{0:T(1024)S(1)} collective-permute-done((f32[4097]{0:T(1024)S(1)}, f32[4097]{0:T(1024)S(1)}, u32[]{:S(2)}, u32[]{:S(2)}) %collective-permute-start) | collective-permute-done | bytes 16420 | tf_op jit(solution)/shard_map/ppermute | solution.py:46
  57.1 4.7 %collective-permute-start.1 = (f32[4097]{0:T(1024)S(1)}, f32[4097]{0:T(1024)S(1)}, u32[]{:S(2)}, u32[]{:S(2)}) collective-permute-start(f32[4097]{0:T(1024)S(1)} %fusion.191), channel_id=1, source_target_pairs={{0,16},{8,24},{16,0},{24,8},{1,17},{9,25},{17,1},{25,9},{2,18},{10... | collective-permute-start | bytes 49172 | tf_op jit(solution)/shard_map/ppermute | solution.py:46
  61.8 3.6 collective-permute-done.7
  68.9 12.3 %collective-permute-done.2 = f32[4097]{0:T(1024)S(1)} collective-permute-done((f32[4097]{0:T(1024)S(1)}, f32[4097]{0:T(1024)S(1)}, u32[]{:S(2)}, u32[]{:S(2)}) %collective-permute-start.2) | collective-permute-done | bytes 16420 | tf_op jit(solution)/shard_map/ppermute | solution.py:46
  89.2 3.2 collective-permute-done.4
  102.9 6.4 %collective-permute-done.21 = bf16[128,2048]{1,0:T(8,128)(2,1)S(1)} collective-permute-done((bf16[128,2048]{1,0:T(8,128)(2,1)}, bf16[128,2048]{1,0:T(8,128)(2,1)S(1)}, u32[]{:S(2)}, u32[]{:S(2)}) %collective-permute-start.21) | collective-permute-done | bytes 524320 | tf_op jit(solution)/shard_map/ppermute | solution.py:57
  124.3 8.3 %collective-permute-done.9 = bf16[512,512]{1,0:T(8,128)(2,1)} collective-permute-done((bf16[512,512]{1,0:T(8,128)(2,1)}, bf16[512,512]{1,0:T(8,128)(2,1)}, u32[]{:S(2)}, u32[]{:S(2)}) %collective-permute-start.9) | collective-permute-done | bytes 524320 | tf_op jit(solution)/shard_map/ppermute | solution.py:54
  132.6 7.2 %collective-permute-done.10 = bf16[512,512]{1,0:T(8,128)(2,1)} collective-permute-done((bf16[512,512]{1,0:T(8,128)(2,1)}, bf16[512,512]{1,0:T(8,128)(2,1)}, u32[]{:S(2)}, u32[]{:S(2)}) %collective-permute-start.10) | collective-permute-done | bytes 524320 | tf_op jit(solution)/shard_map/ppermute | solution.py:56
  150.4 3.6 collective-permute-done.13
  158.9 3.5 fusion.35
  166.0 18.1 %all_to_all.65 = bf16[4,32,2048]{2,1,0:T(8,128)(2,1)} all-to-all(bf16[4,32,2048]{2,1,0:T(8,128)(2,1)S(1)} %bitcast.86), channel_id=1, replica_groups=mesh['z'=4,'y'=2,'x'=2,'c'=2] {'z'}, dimensions={0} | all-to-all | bytes 1048576 | tf_op jit(solution)/shard_map/all_to_all | solution.py:78
  185.3 15.8 %all_gather.20 = bf16[128,2048]{1,0:T(8,128)(2,1)S(1)} all-gather(bf16[32,2048]{1,0:T(8,128)(2,1)S(1)} %reduce_sum.112), channel_id=1, replica_groups=mesh['z'=4,'y'=2,'x'=2,'c'=2] {'z'}, dimensions={0}, use_global_device_ids=true | all-gather | bytes 655360 | tf_op jit(solution)/shard_map/all_gather | solution.py:88
  215.1 4.1 all-to-all-start.2
  230.8 3.6 all-to-all-done.2
  235.5 15.7 %all_gather.21 = bf16[128,2048]{1,0:T(8,128)(2,1)S(1)} all-gather(bf16[32,2048]{1,0:T(8,128)(2,1)S(1)} %reduce_sum.113), channel_id=1, replica_groups=mesh['z'=4,'y'=2,'x'=2,'c'=2] {'z'}, dimensions={0}, use_global_device_ids=true | all-gather | bytes 655360 | tf_op jit(solution)/shard_map/all_gather | solution.py:88
  251.3 6.1 %fusion.41 = f32[512,1024]{1,0:T(8,128)S(1)} fusion(bf16[256,2048]{1,0:T(8,128)(2,1)} %copy-done.5, bf16[256,2048]{1,0:T(8,128)(2,1)} %fusion.13, bf16[256,2048]{1,0:T(8,128)(2,1)} %get-tuple-element.43, bf16[256,2048]{1,0:T(8,128)(2,1)} %get-tuple-element.42, bf16[256,2048]{1,0:T(8,128)(2,1)} %get-tuple-element.41, bf16[256,2048]{1,0:T(8,128)(2,1)} %get-tuple-element.40), kind=kOutput, calls=%fused_computation.59 | convolution fusion | flops 2168455168 | bytes 8388608 | tf_op jit(solution)/shard_map/dot_general | solution.py:32
  268.9 3.7 collective-permute-done.43
  284.0 3.6 collective-permute-done.38
  292.9 3.4 collective-permute-done.46
  348.7 3.5 collective-permute-done.55
  360.5 3.2 fusion.6
  365.6 3.5 all-to-all-start.4
  370.1 3.4 fusion.48
  373.5 5.2 %collective-permute-done.37 = bf16[256,512]{1,0:T(8,128)(2,1)S(1)} collective-permute-done((bf16[256,512]{1,0:T(8,128)(2,1)}, bf16[256,512]{1,0:T(8,128)(2,1)S(1)}, u32[]{:S(2)}, u32[]{:S(2)}) %collective-permute-start.37) | collective-permute-done | bytes 262176 | tf_op jit(solution)/shard_map/ppermute | solution.py:67
  386.9 4.7 %all-to-all-start.3 = ((bf16[4,32,2048]{2,1,0:T(8,128)(2,1)}), bf16[4,32,2048]{2,1,0:T(8,128)(2,1)S(1)}, u32[]{:S(2)}, u32[]{:S(2)}) async-start(bf16[4,32,2048]{2,1,0:T(8,128)(2,1)} %bitcast.85), calls=%async_computation.3 | async-start | bytes 1048576 | tf_op jit(solution)/shard_map/all_to_all | solution.py:78
  393.5 5.8 %add_convert_fusion = bf16[1024,512]{1,0:T(8,128)(2,1)} fusion(f32[1024,512]{1,0:T(8,128)} %fusion.129, f32[1024,512]{1,0:T(8,128)} %fusion.125, f32[1024,512]{1,0:T(8,128)} %fusion.121, f32[1024,512]{1,0:T(8,128)} %fusion.117, f32[1024,512]{1,0:T(8,128)S(1)} %fusion.113, f32[1024,512]{1,0:T(8,128)S(1)} %fusion.91, f32[1024,512]{1,0:T(8,128)S(1)} %copy-done.1, ...), kind=kOutput, calls=%fused_computation.65 | convolution fusion | flops 273678336 | bytes 16515072 | tf_op jit(solution)/shard_map/dot_general | solution.py:28
  399.3 7.1 %all-to-all-done.3 = bf16[4,32,2048]{2,1,0:T(8,128)(2,1)S(1)} async-done(((bf16[4,32,2048]{2,1,0:T(8,128)(2,1)}), bf16[4,32,2048]{2,1,0:T(8,128)(2,1)S(1)}, u32[]{:S(2)}, u32[]{:S(2)}) %all-to-all-start.3) | async-done | bytes 524320 | tf_op jit(solution)/shard_map/all_to_all | solution.py:78
  406.4 3.8 all-to-all-start.5
  410.2 6.3 %fusion.3 = f32[256,2048]{1,0:T(8,128)} fusion(f32[256,2048]{1,0:T(8,128)} %fusion.46, f32[256,2048]{1,0:T(8,128)} %fusion.48, f32[256,2048]{1,0:T(8,128)} %fusion.6, bf16[256,256]{1,0:T(8,128)(2,1)} %collective-permute-done.61, f32[]{:T(128)} %get-tuple-element.87, f32[2048]{0:T(1024)S(1)} %copy-done.42, f32[256]{0:T(256)S(1)} %convert_multiply_fusion, ...), kind=kOutput, calls=%fused_computation.18 | convolution fusion | flops 278396928 | bytes 8538120 | tf_op jit(solution)/shard_map/dot_general | solution.py:28
  417.6 6.5 %all_gather.22 = bf16[128,2048]{1,0:T(8,128)(2,1)S(1)} all-gather(bf16[32,2048]{1,0:T(8,128)(2,1)S(1)} %add_convert_fusion.2), channel_id=1, replica_groups=mesh['z'=4,'y'=2,'x'=2,'c'=2] {'x','c'}, dimensions={0}, use_global_device_ids=true | all-gather | bytes 655360 | tf_op jit(solution)/shard_map/all_gather | solution.py:280
  424.1 7.3 %all_gather.23 = bf16[128,2048]{1,0:T(8,128)(2,1)S(1)} all-gather(bf16[32,2048]{1,0:T(8,128)(2,1)S(1)} %reduce_sum.115), channel_id=1, replica_groups=mesh['z'=4,'y'=2,'x'=2,'c'=2] {'x','c'}, dimensions={0}, use_global_device_ids=true | all-gather | bytes 655360 | tf_op jit(solution)/shard_map/all_gather | solution.py:281
  (357 shorter events, 212.9 us)
Async XLA Ops:
  7.2 115.8 %all-gather.3.cloned.1.call-start = ((), (), s32[]{:S(2)}) async-start(), calls=%async_computation.6 | async-start | bytes 1310720 | tf_op jit(solution)/shard_map/all_gather | solution.py:140
  9.6 91.2 %collective-permute-start.19 = (bf16[128,2048]{1,0:T(8,128)(2,1)}, bf16[128,2048]{1,0:T(8,128)(2,1)}, u32[]{:S(2)}, u32[]{:S(2)}) collective-permute-start(bf16[128,2048]{1,0:T(8,128)(2,1)} %get-tuple-element.71), channel_id=1, source_target_pairs={{0,2},{2,0},{1,3},{3,1},{4,6},{6,4},{5,7},{7,5},{8,10},{10,8},{9,1... | collective-permute-start | bytes 1572872 | tf_op jit(solution)/shard_map/ppermute | solution.py:55
  12.5 84.5 %collective-permute-start.17 = (bf16[128,2048]{1,0:T(8,128)(2,1)}, bf16[128,2048]{1,0:T(8,128)(2,1)}, u32[]{:S(2)}, u32[]{:S(2)}) collective-permute-start(bf16[128,2048]{1,0:T(8,128)(2,1)} %get-tuple-element.71), channel_id=1, source_target_pairs={{0,4},{4,0},{1,5},{5,1},{2,6},{6,2},{3,7},{7,3},{8,12},{12,8},{9,1... | collective-permute-start | bytes 1572872 | tf_op jit(solution)/shard_map/ppermute | solution.py:54
  14.3 15.1 %collective-permute-start.6 = (s32[128]{0:T(128)S(1)}, s32[128]{0:T(128)S(1)}, u32[]{:S(2)}, u32[]{:S(2)}) collective-permute-start(s32[128]{0:T(128)S(1)} %select_n.191), channel_id=1, source_target_pairs={{0,8},{8,0},{16,24},{24,16},{1,9},{9,1},{17,25},{25,17},{2,10},{10... | collective-permute-start | bytes 1544 | tf_op jit(solution)/shard_map/ppermute | solution.py:46
  19.0 93.3 %all-to-all-start = ((bf16[256,4,512]{0,2,1:T(8,128)(2,1)}), bf16[256,4,512]{0,2,1:T(8,128)(2,1)S(1)}, u32[]{:S(2)}, u32[]{:S(2)}) async-start(bf16[256,4,512]{0,2,1:T(8,128)(2,1)} %bitcast.72), calls=%async_computation | async-start | bytes 2097152 | tf_op jit(solution)/shard_map/all_to_all | solution.py:126
  26.1 30.3 %collective-permute-start = (f32[4097]{0:T(1024)S(1)}, f32[4097]{0:T(1024)S(1)}, u32[]{:S(2)}, u32[]{:S(2)}) collective-permute-start(f32[4097]{0:T(1024)S(1)} %pad_maximum_fusion.18), channel_id=1, source_target_pairs={{0,8},{8,0},{16,24},{24,16},{1,9},{9,1},{17,25},{25,17},{2,10},{10... | collective-permute-start | bytes 49172 | tf_op jit(solution)/shard_map/ppermute | solution.py:46
  28.2 72.0 %collective-permute-start.20 = (bf16[128,2048]{1,0:T(8,128)(2,1)}, bf16[128,2048]{1,0:T(8,128)(2,1)}, u32[]{:S(2)}, u32[]{:S(2)}) collective-permute-start(bf16[128,2048]{1,0:T(8,128)(2,1)} %get-tuple-element.70), channel_id=1, source_target_pairs={{0,2},{2,0},{1,3},{3,1},{4,6},{6,4},{5,7},{7,5},{8,10},{10,8},{9,1... | collective-permute-start | bytes 1572872 | tf_op jit(solution)/shard_map/ppermute | solution.py:53
  29.4 36.1 %collective-permute-start.7 = (s32[128]{0:T(128)S(1)}, s32[128]{0:T(128)S(1)}, u32[]{:S(2)}, u32[]{:S(2)}) collective-permute-start(s32[128]{0:T(128)S(1)} %add.282), channel_id=1, source_target_pairs={{0,16},{8,24},{16,0},{24,8},{1,17},{9,25},{17,1},{25,9},{2,18},{10... | collective-permute-start | bytes 1544 | tf_op jit(solution)/shard_map/ppermute | solution.py:46
  66.2 32.5 %collective-permute-start.18 = (bf16[128,2048]{1,0:T(8,128)(2,1)}, bf16[128,2048]{1,0:T(8,128)(2,1)S(1)}, u32[]{:S(2)}, u32[]{:S(2)}) collective-permute-start(bf16[128,2048]{1,0:T(8,128)(2,1)} %get-tuple-element.70), channel_id=1, source_target_pairs={{0,4},{4,0},{1,5},{5,1},{2,6},{6,2},{3,7},{7,3},{8,12},{12,8},{9,1... | collective-permute-start | bytes 1572872 | tf_op jit(solution)/shard_map/ppermute | solution.py:56
  117.4 15.2 %collective-permute-start.9 = (bf16[512,512]{1,0:T(8,128)(2,1)}, bf16[512,512]{1,0:T(8,128)(2,1)}, u32[]{:S(2)}, u32[]{:S(2)}) collective-permute-start(bf16[512,512]{1,0:T(8,128)(2,1)} %bitcast.11), channel_id=1, source_target_pairs={{0,4},{4,0},{1,5},{5,1},{2,6},{6,2},{3,7},{7,3},{8,12},{12,8},{9,1... | collective-permute-start | bytes 1572872 | tf_op jit(solution)/shard_map/ppermute | solution.py:54
  117.9 21.9 %collective-permute-start.10 = (bf16[512,512]{1,0:T(8,128)(2,1)}, bf16[512,512]{1,0:T(8,128)(2,1)}, u32[]{:S(2)}, u32[]{:S(2)}) collective-permute-start(bf16[512,512]{1,0:T(8,128)(2,1)} %bitcast.12), channel_id=1, source_target_pairs={{0,4},{4,0},{1,5},{5,1},{2,6},{6,2},{3,7},{7,3},{8,12},{12,8},{9,1... | collective-permute-start | bytes 1572872 | tf_op jit(solution)/shard_map/ppermute | solution.py:56
  120.9 27.3 %collective-permute-start.11 = (bf16[512,512]{1,0:T(8,128)(2,1)}, bf16[512,512]{1,0:T(8,128)(2,1)}, u32[]{:S(2)}, u32[]{:S(2)}) collective-permute-start(bf16[512,512]{1,0:T(8,128)(2,1)} %bitcast.11), channel_id=1, source_target_pairs={{0,2},{2,0},{1,3},{3,1},{4,6},{6,4},{5,7},{7,5},{8,10},{10,8},{9,1... | collective-permute-start | bytes 1572872 | tf_op jit(solution)/shard_map/ppermute | solution.py:55
  122.4 22.6 %collective-permute-start.12 = (bf16[512,512]{1,0:T(8,128)(2,1)}, bf16[512,512]{1,0:T(8,128)(2,1)}, u32[]{:S(2)}, u32[]{:S(2)}) collective-permute-start(bf16[512,512]{1,0:T(8,128)(2,1)} %bitcast.12), channel_id=1, source_target_pairs={{0,2},{2,0},{1,3},{3,1},{4,6},{6,4},{5,7},{7,5},{8,10},{10,8},{9,1... | collective-permute-start | bytes 1572872 | tf_op jit(solution)/shard_map/ppermute | solution.py:53
  124.2 32.3 %collective-permute-start.5 = (bf16[128,2048]{1,0:T(8,128)(2,1)S(1)}, bf16[128,2048]{1,0:T(8,128)(2,1)}, u32[]{:S(2)}, u32[]{:S(2)}) collective-permute-start(bf16[128,2048]{1,0:T(8,128)(2,1)S(1)} %get-tuple-element.69), channel_id=1, source_target_pairs={{0,1},{1,0},{2,3},{3,2},{4,5},{5,4},{6,7},{7,6},{8,9},{9,8},{10,11... | collective-permute-start | bytes 1572872 | tf_op jit(solution)/shard_map/ppermute | solution.py:84
  215.1 19.3 %all-to-all-start.2 = ((bf16[4,32,2048]{2,1,0:T(8,128)(2,1)}), bf16[4,32,2048]{2,1,0:T(8,128)(2,1)}, u32[]{:S(2)}, u32[]{:S(2)}) async-start(bf16[4,32,2048]{2,1,0:T(8,128)(2,1)} %bitcast.84), calls=%async_computation.2 | async-start | bytes 1048576 | tf_op jit(solution)/shard_map/all_to_all | solution.py:78
  225.0 53.8 %collective-permute-start.44 = (bf16[128,1024]{1,0:T(8,128)(2,1)}, bf16[128,1024]{1,0:T(8,128)(2,1)}, u32[]{:S(2)}, u32[]{:S(2)}) collective-permute-start(bf16[128,1024]{1,0:T(8,128)(2,1)} %pad_maximum_fusion.7), channel_id=1, source_target_pairs={{0,6},{2,4},{4,2},{6,0},{1,7},{3,5},{5,3},{7,1},{8,14},{10,12},{12... | collective-permute-start | bytes 786440 | tf_op jit(solution)/shard_map/ppermute | solution.py:67
  226.4 40.9 %collective-permute-start.41 = (bf16[128,1024]{1,0:T(8,128)(2,1)}, bf16[128,1024]{1,0:T(8,128)(2,1)}, u32[]{:S(2)}, u32[]{:S(2)}) collective-permute-start(bf16[128,1024]{1,0:T(8,128)(2,1)} %pad_maximum_fusion.7), channel_id=1, source_target_pairs={{0,4},{4,0},{1,5},{5,1},{2,6},{6,2},{3,7},{7,3},{8,12},{12,8},{9,1... | collective-permute-start | bytes 786440 | tf_op jit(solution)/shard_map/ppermute | solution.py:66
  228.8 63.1 %collective-permute-start.59 = (bf16[128,2048]{1,0:T(8,128)(2,1)}, bf16[128,2048]{1,0:T(8,128)(2,1)}, u32[]{:S(2)}, u32[]{:S(2)}) collective-permute-start(bf16[128,2048]{1,0:T(8,128)(2,1)} %slice.199), channel_id=1, source_target_pairs={{0,6},{2,4},{4,2},{6,0},{1,7},{3,5},{5,3},{7,1},{8,14},{10,12},{12... | collective-permute-start | bytes 1572872 | tf_op jit(solution)/shard_map/ppermute | solution.py:67
  229.3 63.1 %collective-permute-start.56 = (bf16[128,2048]{1,0:T(8,128)(2,1)}, bf16[128,2048]{1,0:T(8,128)(2,1)}, u32[]{:S(2)}, u32[]{:S(2)}) collective-permute-start(bf16[128,2048]{1,0:T(8,128)(2,1)} %slice.199), channel_id=1, source_target_pairs={{0,4},{4,0},{1,5},{5,1},{2,6},{6,2},{3,7},{7,3},{8,12},{12,8},{9,1... | collective-permute-start | bytes 1572872 | tf_op jit(solution)/shard_map/ppermute | solution.py:66
  267.3 25.2 %collective-permute-start.53 = (bf16[128,2048]{1,0:T(8,128)(2,1)}, bf16[128,2048]{1,0:T(8,128)(2,1)}, u32[]{:S(2)}, u32[]{:S(2)}) collective-permute-start(bf16[128,2048]{1,0:T(8,128)(2,1)} %slice.199), channel_id=1, source_target_pairs={{0,2},{2,0},{1,3},{3,1},{4,6},{6,4},{5,7},{7,5},{8,10},{10,8},{9,1... | collective-permute-start | bytes 1572872 | tf_op jit(solution)/shard_map/ppermute | solution.py:65
  291.9 52.3 %collective-permute-start.60 = (bf16[128,2048]{1,0:T(8,128)(2,1)}, bf16[128,2048]{1,0:T(8,128)(2,1)}, u32[]{:S(2)}, u32[]{:S(2)}) collective-permute-start(bf16[128,2048]{1,0:T(8,128)(2,1)} %collective-permute-done.59), channel_id=1, source_target_pairs={{0,1},{1,0},{2,3},{3,2},{4,5},{5,4},{6,7},{7,6},{8,9},{9,8},{10,11... | collective-permute-start | bytes 1572872 | tf_op jit(solution)/shard_map/ppermute | solution.py:84
  292.4 56.2 %collective-permute-start.57 = (bf16[128,2048]{1,0:T(8,128)(2,1)}, bf16[128,2048]{1,0:T(8,128)(2,1)}, u32[]{:S(2)}, u32[]{:S(2)}) collective-permute-start(bf16[128,2048]{1,0:T(8,128)(2,1)} %collective-permute-done.56), channel_id=1, source_target_pairs={{0,1},{1,0},{2,3},{3,2},{4,5},{5,4},{6,7},{7,6},{8,9},{9,8},{10,11... | collective-permute-start | bytes 1572872 | tf_op jit(solution)/shard_map/ppermute | solution.py:84
  292.5 61.9 %collective-permute-start.54 = (bf16[128,2048]{1,0:T(8,128)(2,1)}, bf16[128,2048]{1,0:T(8,128)(2,1)}, u32[]{:S(2)}, u32[]{:S(2)}) collective-permute-start(bf16[128,2048]{1,0:T(8,128)(2,1)} %collective-permute-done.53), channel_id=1, source_target_pairs={{0,1},{1,0},{2,3},{3,2},{4,5},{5,4},{6,7},{7,6},{8,9},{9,8},{10,11... | collective-permute-start | bytes 1572872 | tf_op jit(solution)/shard_map/ppermute | solution.py:84
  303.1 65.9 %collective-permute-start.35 = (bf16[128,1024]{1,0:T(8,128)(2,1)}, bf16[128,1024]{1,0:T(8,128)(2,1)}, u32[]{:S(2)}, u32[]{:S(2)}) collective-permute-start(bf16[128,1024]{1,0:T(8,128)(2,1)} %pad_maximum_fusion.13), channel_id=1, source_target_pairs={{0,6},{2,4},{4,2},{6,0},{1,7},{3,5},{5,3},{7,1},{8,14},{10,12},{12... | collective-permute-start | bytes 786440 | tf_op jit(solution)/shard_map/ppermute | solution.py:67
  344.2 38.8 %collective-permute-start.32 = (bf16[128,1024]{1,0:T(8,128)(2,1)}, bf16[128,1024]{1,0:T(8,128)(2,1)}, u32[]{:S(2)}, u32[]{:S(2)}) collective-permute-start(bf16[128,1024]{1,0:T(8,128)(2,1)} %pad_maximum_fusion.13), channel_id=1, source_target_pairs={{0,4},{4,0},{1,5},{5,1},{2,6},{6,2},{3,7},{7,3},{8,12},{12,8},{9,1... | collective-permute-start | bytes 786440 | tf_op jit(solution)/shard_map/ppermute | solution.py:66
  348.6 15.1 %collective-permute-start.28 = (bf16[128,2048]{1,0:T(8,128)(2,1)S(1)}, bf16[128,2048]{1,0:T(8,128)(2,1)S(1)}, u32[]{:S(2)}, u32[]{:S(2)}) collective-permute-start(bf16[128,2048]{1,0:T(8,128)(2,1)S(1)} %copy-done.36), channel_id=1, source_target_pairs={{0,1},{1,0},{2,3},{3,2},{4,5},{5,4},{6,7},{7,6},{8,9},{9,8},{10,11... | collective-permute-start | bytes 1572872 | tf_op jit(solution)/shard_map/ppermute | solution.py:73
  354.4 30.1 %collective-permute-start.29 = (bf16[128,1024]{1,0:T(8,128)(2,1)}, bf16[128,1024]{1,0:T(8,128)(2,1)S(1)}, u32[]{:S(2)}, u32[]{:S(2)}) collective-permute-start(bf16[128,1024]{1,0:T(8,128)(2,1)} %pad_maximum_fusion.16), channel_id=1, source_target_pairs={{0,2},{2,0},{1,3},{3,1},{4,6},{6,4},{5,7},{7,5},{8,10},{10,8},{9,1... | collective-permute-start | bytes 786440 | tf_op jit(solution)/shard_map/ppermute | solution.py:65
  358.8 25.7 %collective-permute-start.26 = (bf16[128,2048]{1,0:T(8,128)(2,1)}, bf16[128,2048]{1,0:T(8,128)(2,1)}, u32[]{:S(2)}, u32[]{:S(2)}) collective-permute-start(bf16[128,2048]{1,0:T(8,128)(2,1)} %slice.295), channel_id=1, source_target_pairs={{0,1},{1,0},{2,3},{3,2},{4,5},{5,4},{6,7},{7,6},{8,9},{9,8},{10,11... | collective-permute-start | bytes 1572872 | tf_op jit(solution)/shard_map/ppermute | solution.py:73
  365.6 21.4 %all-to-all-start.4 = ((bf16[4,32,2048]{2,1,0:T(8,128)(2,1)}), bf16[4,32,2048]{2,1,0:T(8,128)(2,1)S(1)}, u32[]{:S(2)}, u32[]{:S(2)}) async-start(bf16[4,32,2048]{2,1,0:T(8,128)(2,1)} %bitcast.26), calls=%async_computation.4 | async-start | bytes 1048576 | tf_op jit(solution)/shard_map/all_to_all | solution.py:78
  383.0 27.2 %collective-permute-start.61 = (bf16[256,256]{1,0:T(8,128)(2,1)S(1)}, bf16[256,256]{1,0:T(8,128)(2,1)}, u32[]{:S(2)}, u32[]{:S(2)}) collective-permute-start(bf16[256,256]{1,0:T(8,128)(2,1)S(1)} %get-tuple-element.74), channel_id=1, source_target_pairs={{0,2},{2,0},{1,3},{3,1},{4,6},{6,4},{5,7},{7,5},{8,10},{10,8},{9,1... | collective-permute-start | bytes 393224 | tf_op jit(solution)/shard_map/ppermute | solution.py:65
  386.9 19.4 %all-to-all-start.3 = ((bf16[4,32,2048]{2,1,0:T(8,128)(2,1)}), bf16[4,32,2048]{2,1,0:T(8,128)(2,1)S(1)}, u32[]{:S(2)}, u32[]{:S(2)}) async-start(bf16[4,32,2048]{2,1,0:T(8,128)(2,1)} %bitcast.85), calls=%async_computation.3 | async-start | bytes 1048576 | tf_op jit(solution)/shard_map/all_to_all | solution.py:78
  406.4 29.0 %all-to-all-start.5 = ((bf16[4,256,512]{2,1,0:T(8,128)(2,1)}), bf16[4,256,512]{2,1,0:T(8,128)(2,1)S(1)}, u32[]{:S(2)}, u32[]{:S(2)}) async-start(bf16[4,256,512]{2,1,0:T(8,128)(2,1)} %bitcast.31), calls=%async_computation.5 | async-start | bytes 2097152 | tf_op jit(solution)/shard_map/all_to_all | solution.py:255
  (89 other events, 643.8 us)
Sparse Core Ops, SparseCore 0:
  17.7 45.7 all-gather.2
where the time goes:
time: 456 us; the launch traced here: 447 us
  waiting for transfers between devices  129 us (28%)
  starting transfers between devices  82 us (18%)
  matrix products  63.6 us (14%)
  blocking collectives  63.4 us (14%)
  other arithmetic  48.1 us (11%)
  local copies, waits for them, and re-layouts  42.2 us (9%)
  between operations  18.2 us (4%)
    ppermute x10, waiting for transfers between devices, sum_over(): values = values + lax.ppermute(values, name, pairs)  51.1 us
    dot_general x16, matrix products, contract_rows(): lax.dot_general(left, right, (((0,), (0,)), ((), ())), preferred_element_...  42.8 us
    all_gather x2, blocking collectives, gather_rows(): return with_other_core(lax.all_gather(quarter, 'z', axis=0, tiled=True))  31.5 us
    all_to_all x1, blocking collectives, sum_planes(): got = lax.all_to_all(rows, 'z', 0, 0, tiled=True)  18.1 us
    ppermute x10, starting transfers between devices, sum_over(): values = values + lax.ppermute(values, name, pairs)  14.7 us
    unnamed x105, local copies, waits for them, and re-layouts  14 us
    dot_general x8, matrix products, times(): return jnp.dot(left, right, preferred_element_type=F32)  13.2 us
    all_to_all x3, starting transfers between devices, sum_planes(): got = lax.all_to_all(rows, 'z', 0, 0, tiled=True)  12.3 us
  transfers between devices with their start and end apart: 73, of which 31 were waited for; matrix products, arithmetic and copies ran while one was open for 29% of the time, Pallas kernels for 0%

commit v1 on v0

v1 whole, which is shorter than its diff:
```python
import jax
import jax.numpy as jnp
from jax import lax
from jax.sharding import Mesh
from jax.sharding import PartitionSpec as P

F32 = jnp.float32
BF16 = jnp.bfloat16
EVERY = ("z", "y", "x", "c")
SWAP = [(0, 1), (1, 0)]


def probe_signs(seeds, width):
    columns = jnp.arange(width, dtype=jnp.int32)
    mixed = seeds[:, None] * 747796405 + columns[None, :] * 1640531527
    mixed = mixed ^ lax.shift_right_logical(mixed, jnp.full_like(mixed, 16))
    mixed = mixed * 668265261
    mixed = mixed ^ lax.shift_right_logical(mixed, jnp.full_like(mixed, 15))
    lowbit = jnp.bitwise_and(lax.shift_right_logical(mixed, jnp.full_like(mixed, 7)), 1)
    return (1 - 2 * lowbit).astype(F32).astype(BF16)


def times(left, right):
    return jnp.dot(left, right, preferred_element_type=F32)


def contract_rows(left, right):
    return lax.dot_general(left, right, (((0,), (0,)), ((), ())), preferred_element_type=F32)


def contract_cols(left, right):
    return lax.dot_general(left, right, (((1,), (1,)), ((), ())), preferred_element_type=F32)


def in_order(own, other, index):
    first = jnp.where(index == 0, own, other)
    second = jnp.where(index == 0, other, own)
    return jnp.concatenate([first, second], 0)


def sum_over(values, names):
    for name in names:
        size, step = lax.axis_size(name), 1
        while step < size:
            pairs = [(place, place ^ step) for place in range(size)]
            values = values + lax.ppermute(values, name, pairs)
            step *= 2
    return values


tied = lax.optimization_barrier


def spread(block, *later):
    half = block.shape[0] // 2
    x_low = lax.ppermute(block[half:], "x", SWAP)
    y_top = lax.ppermute(block[:half], "y", SWAP)
    x_top = lax.ppermute(block[:half], "x", SWAP)
    y_low = lax.ppermute(block[half:], "y", SWAP)
    x_low, y_top, later = tied((x_low, y_top, later))
    far_top = lax.ppermute(y_top, "x", SWAP)
    far_low = lax.ppermute(x_low, "y", SWAP)
    stack = lambda top, low: jnp.concatenate([top, low], 0)
    blocks = stack(x_top, x_low), stack(y_top, y_low), stack(far_top, far_low)
    return blocks, later


def exchange(to_x, to_y, across):
    return (
        lax.ppermute(to_x, "x", SWAP),
        lax.ppermute(to_y, "y", SWAP),
        lax.ppermute(across, ("y", "x"), [(place, 3 - place) for place in range(4)]),
    )


def fold_cores(part):
    half = part.shape[0] // 2
    got = lax.ppermute(part[half:].astype(BF16), "c", SWAP)
    return (part[:half] + got.astype(F32)).astype(BF16)


def sum_planes(*parts):
    planes = lax.axis_size("z")
    rows = jnp.stack([part.reshape(planes, -1, part.shape[1]) for part in parts], 1)
    got = lax.all_to_all(rows, "z", 0, 0, tiled=True)
    return jnp.sum(got.astype(F32), 0)


def with_other_core(half):
    return jnp.concatenate([half, lax.ppermute(half, "c", SWAP)], 0)


def gather_rows(quarter):
    return with_other_core(lax.all_gather(quarter, "z", axis=0, tiled=True))


def on_device(tokens, cotangent, probe_seed, w_in, bias, w_out, left_in, left_out):
    coef = 0.9
    planes = lax.axis_size("z")
    at_z, at_y, at_x, core = (lax.axis_index(name) for name in EVERY)
    count, width = tokens.shape
    rows_in, hid_rep = w_in.shape
    rows_out = w_out.shape[0]
    piece = hid_rep // planes
    quarter = count // 4
    at_dp = at_z * 2 + at_y
    at_rep = at_x * 2 + core

    def own_quarter(array):
        return lax.dynamic_slice_in_dim(array, at_rep * quarter, quarter, 0)

    def rows_of(array, y_index):
        starts = [(2 * plane + y_index) * rows_in for plane in range(planes)]
        return jnp.concatenate(
            [lax.dynamic_slice_in_dim(array, start, rows_in, 1) for start in starts], 1
        )

    def units_of(array, y_index, x_other):
        start = (2 * x_other + y_index) * rows_out
        return lax.dynamic_slice_in_dim(array, start, rows_out, 1)

    left_one = left_in.astype(F32)
    slice_one = lax.dynamic_slice_in_dim(left_in, at_dp * rows_in, rows_in, 0)
    slice_two = lax.dynamic_slice_in_dim(left_out, at_dp * rows_out, rows_out, 0)
    p_part = times(slice_one, w_in)
    q_part = times(slice_two, w_out)
    slice_one = slice_one.astype(F32)
    slice_two = slice_two.astype(F32)
    sums = sum_over(
        jnp.concatenate([p_part, q_part, jnp.sum(slice_two * slice_two)[None]]), ("z",)
    )

    seeds = jnp.where(
        jnp.arange(planes)[:, None] == at_z, own_quarter(probe_seed)[None, :], 0
    ).reshape(-1)
    seeds = sum_over(seeds, ("z",))
    w_late, sums, seeds = tied((w_in, sums, seeds))
    in_z = lax.all_to_all(w_late, "z", 1, 0, tiled=True)
    bias_own = lax.dynamic_slice_in_dim(bias, at_z * piece, piece, 0)
    (out_x, out_y, out_d), (sums, seeds, bias_own) = spread(w_out, sums, seeds, bias_own)
    full_out = jnp.concatenate([in_order(w_out, out_y, at_y), in_order(out_x, out_d, at_y)], 0)

    def join_rows(own, other):
        first = jnp.where(at_y == 0, own, other).reshape(planes, 1, rows_in, piece)
        second = jnp.where(at_y == 0, other, own).reshape(planes, 1, rows_in, piece)
        return jnp.concatenate([first, second], 1).reshape(width, piece)

    tok_own = own_quarter(tokens)
    in_z, pair = tied((in_z, jnp.stack([tok_own, own_quarter(cotangent)])))
    (in_x, in_y, in_d), _ = spread(in_z)
    full_in = jnp.concatenate([join_rows(in_z, in_y), join_rows(in_x, in_d)], 1)

    sums = sum_over(sums, ("y",))
    p_vec = sums[:hid_rep]
    sums = sum_over(jnp.concatenate([sums[hid_rep:], jnp.sum(p_vec * p_vec)[None]]), ("c", "x"))
    q_vec = sums[:width]
    p_norm = sums[-1]
    q_norm = jnp.sum(q_vec * q_vec)
    scale_in = coef * jnp.sqrt(jnp.sum(left_one * left_one) / p_norm)
    scale_out = coef * jnp.sqrt(sums[-2] / q_norm)

    pair = lax.all_gather(pair, "z", axis=1)
    tok = with_other_core(pair[0].reshape(-1, width))
    cot = with_other_core(pair[1].reshape(-1, width))
    n = tok.shape[0]
    seeds = with_other_core(seeds)
    probe = probe_signs(seeds, width)
    bias_all = jnp.concatenate([bias_own, lax.ppermute(bias_own, "x", SWAP)])

    raw = times(jnp.concatenate([tok, probe], 0), full_in)
    raw_z = raw[:n]
    e_one = scale_in * raw[n:]
    tanh_z = jnp.tanh(scale_in * raw_z + bias_all)
    deriv = 1.0 - tanh_z * tanh_z
    act = tanh_z.astype(BF16)
    r_one = (e_one * deriv).astype(BF16)
    factors = n <= 4 * rows_out

    def exchange_units(array):
        parts = exchange(
            units_of(array, at_y, 1), units_of(array, 1 - at_y, 0), units_of(array, 1 - at_y, 1)
        )
        return (units_of(array, at_y, 0), *parts)

    j_pair = fold_cores(scale_out * times(r_one, full_out))
    j_pair, cot_late, seeds_late, probe_late, act_late = tied((j_pair, cot, seeds, probe, act))
    if factors:
        cot_rows = lax.all_gather(cot_late, ("x", "y"), axis=0, tiled=True)
        seeds_all = jnp.where(
            jnp.arange(4)[:, None] == at_x * 2 + at_y, seeds_late[None, :], 0
        ).reshape(-1)
        seeds_all = sum_over(seeds_all, ("x", "y")).reshape(4, n)
        act_units = exchange_units(act_late)
    backs = contract_cols(jnp.concatenate([probe_late, cot_late], 0), full_out)
    raw_b = backs[:n]
    raw_c = backs[n:]
    hd = deriv * (scale_out * raw_b)
    h_round = hd.astype(BF16)
    quarter_one = sum_planes(j_pair)[0].astype(BF16)
    quarter_one, h_round, raw_c = tied((quarter_one, h_round, raw_c))
    j_one = gather_rows(quarter_one)

    e_two = scale_in * times(j_one, full_in)
    r_two = (e_two * deriv).astype(BF16)
    j_pair = fold_cores(scale_out * times(r_two, full_out))
    j_pair, act_late = tied((j_pair, act_late))
    branch = fold_cores(scale_out * times(act_late, full_out))
    quarter_two = sum_planes(j_pair)[0].astype(BF16)
    if factors:
        quarter_two, branch, seeds_all, cot_rows, act_units = tied(
            (quarter_two, branch, seeds_all, cot_rows, act_units)
        )
    else:
        quarter_two, branch = tied((quarter_two, branch))
    j_two, branch = tied((gather_rows(quarter_two), branch))

    w_vec = (probe.astype(F32) - j_one.astype(F32) + j_two.astype(F32)).astype(BF16)
    e_three = scale_in * times(j_two, full_in)
    a_vec = e_one - e_two + e_three
    second = -2.0 * tanh_z * deriv
    dz_vec = scale_out * raw_c * deriv - a_vec * (scale_out * raw_b) * second
    dz_round = dz_vec.astype(BF16)
    g_round = (a_vec * deriv).astype(BF16)

    left_grad = jnp.concatenate([tok, w_vec], 0)
    right_grad = jnp.concatenate([dz_round, -h_round], 0)
    own_cols, other_cols = right_grad[:, :piece], right_grad[:, piece:]
    near, over = rows_of(left_grad, at_y), rows_of(left_grad, 1 - at_y)
    half = near.shape[1] // 2
    near_top, near_low = near[:, :half], near[:, half:]
    over_top, over_low = over[:, :half], over[:, half:]
    across_x = contract_rows(over_top, other_cols).astype(BF16)
    across_y = contract_rows(over_low, other_cols).astype(BF16)
    across_x, across_y, own_cols, other_cols = tied((across_x, across_y, own_cols, other_cols))
    across_x = lax.ppermute(across_x, "x", SWAP)
    across_y = lax.ppermute(across_y, "y", SWAP)
    x_top = lax.ppermute(contract_rows(near_top, other_cols).astype(BF16), "x", SWAP)
    y_low = lax.ppermute(contract_rows(over_low, own_cols).astype(BF16), "y", SWAP)
    dx = fold_cores(scale_in * contract_cols(dz_round, full_in))
    ends = sum_planes(branch, dx)
    ends = jnp.stack([tok_own.astype(F32) + ends[0], ends[1]]).astype(BF16)
    across_x, across_y, g_late, a_late, e_late, dz_late = tied(
        (across_x, across_y, g_round, a_vec, e_three, dz_round)
    )
    terms = jnp.sum((e_one - e_two / 2.0 + e_late / 3.0) * hd, axis=1)
    inner_one = jnp.sum(dz_late.astype(F32) * raw_z - h_round.astype(F32) * (a_late / scale_in))
    inner_two = jnp.sum(act.astype(F32) * raw_c - g_late.astype(F32) * raw_b)
    inner = jnp.stack([inner_one, inner_two])
    tail = jnp.concatenate([terms, inner])
    got = lax.ppermute(tail, "c", SWAP)
    got = jnp.concatenate([got[n // 2 : n], got[: n // 2], got[n:]])
    tail = sum_over(tail + got, ("z",))
    ends = lax.all_gather(ends, ("x", "c"), axis=1, tiled=True)

    x_low = contract_rows(near_low, other_cols) + across_y.astype(F32)
    y_top = contract_rows(over_top, own_cols) + across_x.astype(F32)
    x_low = lax.ppermute(x_low.astype(BF16), "x", SWAP)
    y_top = lax.ppermute(y_top.astype(BF16), "y", SWAP)
    top = contract_rows(near_top, own_cols) + x_top.astype(F32) + y_top.astype(F32)
    low = contract_rows(near_low, own_cols) + x_low.astype(F32) + y_low.astype(F32)
    block = jnp.concatenate([top.astype(BF16), low.astype(BF16)], 0)
    block, tail, g_late = tied((block, tail, g_late))
    grad_one = lax.all_to_all(block, "z", 0, 1, tiled=True).astype(F32)

    if factors:
        own_act, x_act, y_act, d_act = act_units
        act_rows = in_order(
            in_order(own_act, y_act, at_y), in_order(x_act, d_act, at_y), at_x
        )
        grad_two = contract_rows(act_rows, cot_rows)
        at_group = at_x * 2 + at_y
        seeds_near = [
            lax.dynamic_index_in_dim(seeds_all, at_group ^ other, 0, keepdims=False)
            for other in (0, 2, 1, 3)
        ]
        probe_rows = probe_signs(jnp.concatenate(seeds_near), width)
        g_rows = jnp.concatenate(exchange_units(g_late), 0)
        grad_two = grad_two - contract_rows(g_rows, probe_rows)
    else:

        def block_two(y_index, x_other):
            grad = contract_rows(units_of(act, y_index, x_other), cot)
            return grad - contract_rows(units_of(g_late, y_index, x_other), probe)

        parts = exchange(
            block_two(at_y, 1).astype(BF16),
            block_two(1 - at_y, 0).astype(BF16),
            block_two(1 - at_y, 1).astype(BF16),
        )
        grad_two = block_two(at_y, 0) + sum(part.astype(F32) for part in parts)

    output = ends[0]
    grad_tokens = cotangent.astype(F32) + ends[1].astype(F32)

    terms = lax.dynamic_index_in_dim(tail[:n].reshape(2, planes, quarter), at_z, 1, keepdims=False)
    terms = in_order(terms[0], terms[1], core)
    tail = jnp.concatenate([tail[n:], terms])
    tail_x = lax.ppermute(tail, "x", SWAP)
    logdet = in_order(tail[2:], tail_x[2:], at_x)
    inner = sum_over(tail[:2] + tail_x[:2], ("y",))

    grad_in = scale_in * (grad_one - inner[0] * slice_one[:, None] * p_vec[None, :] / p_norm)
    grad_out = scale_out * (grad_two - inner[1] * slice_two[:, None] * q_vec[None, :] / q_norm)
    return (output, logdet, grad_tokens, grad_in, grad_out)


def solution(mesh):
    fine = Mesh(
        mesh.devices.reshape(mesh.shape["dp"] // 2, 2, mesh.shape["rep"] // 2, 2), EVERY
    )
    dp, rep = ("z", "y"), ("x", "c")
    placed = (
        P(dp, None),
        P(dp, None),
        P(dp),
        P(dp, rep),
        P(rep),
        P(rep + dp, None),
        P(),
        P(rep),
    )
    return jax.shard_map(
        on_device,
        mesh=fine,
        in_specs=placed,
        out_specs=(P(dp, None), P(dp), P(dp, None), P(dp, rep), P(rep + dp, None)),
        check_vma=False,
    )
```

time: 456 us -> 322 us (0.71); the launches traced: 447 us -> 321 us
  waiting for transfers between devices: 129 us -> 81.2 us
  blocking collectives: 63.4 us -> 32.1 us
  matrix products: 63.6 us -> 35.3 us
  starting transfers between devices: 82 us -> 62.3 us
  other arithmetic: 48.1 us -> 53.5 us
    ppermute x10 -> x12, waiting for transfers between devices: 51.1 us -> 13.9 us  [sum_over(): values = values + lax.ppermute(values, name, pairs)]
    dot_general x16 -> x10, matrix products: 42.8 us -> 16.4 us  [contract_rows(): lax.dot_general(left, right, (((0,), (0,)), ((), ())), preferred_element_...]
    all_to_all x1 -> x0, blocking collectives: 18.1 us -> none  [sum_planes(): got = lax.all_to_all(rows, 'z', 0, 0, tiled=True)]
    all_gather x2 -> x0, blocking collectives: 13.8 us -> none  [the longest x1 7.28 us: on_device(): dx = lax.all_gather(dx, ('x', 'c'), axis=0, tiled=True)]
    ppermute x2, waiting for transfers between devices: 0.01 us -> 11.9 us  [spread(): x_low = lax.ppermute(block[half:], 'x', SWAP)]
    all_to_all x1, waiting for transfers between devices: 2.9 us -> 14.5 us  [on_device(): grad_one = lax.all_to_all(block, 'z', 0, 1, tiled=True).astype(F32)]
    ppermute x7 -> x2, waiting for transfers between devices: 10 us -> 0.01 us  [exchange(): lax.ppermute(across, ('y', 'x'), [(place, 3 - place) for place in range(4)])]
    ppermute x7 -> x2, starting transfers between devices: 10 us -> 2.39 us  [exchange(): lax.ppermute(across, ('y', 'x'), [(place, 3 - place) for place in range(4)])]
  transfers between devices with their start and end apart: 73 -> 56, of which waited for: 31 -> 19; matrix products, arithmetic and copies ran while one was open for 29% -> 31% of each run, Pallas kernels for 0% -> 0%
where the time goes in v1:
time: 322 us; the launch traced here: 321 us
  waiting for transfers between devices  81.2 us (25%)
  starting transfers between devices  62.3 us (19%)
  other arithmetic  53.5 us (17%)
  local copies, waits for them, and re-layouts  38.6 us (12%)
  matrix products  35.3 us (11%)
  blocking collectives  32.1 us (10%)
  between operations  17.6 us (5%)
    all_gather x2, blocking collectives, gather_rows(): return with_other_core(lax.all_gather(quarter, 'z', axis=0, tiled=True))  32.1 us
    unnamed x119, local copies, waits for them, and re-layouts  17.3 us
    dot_general x10, matrix products, contract_rows(): lax.dot_general(left, right, (((0,), (0,)), ((), ())), preferred_element_...  16.4 us
    all_to_all x1, waiting for transfers between devices, on_device(): grad_one = lax.all_to_all(block, 'z', 0, 1, tiled=True).astype(F32)  14.5 us
    ppermute x12, waiting for transfers between devices, sum_over(): values = values + lax.ppermute(values, name, pairs)  13.9 us
    ppermute x12, starting transfers between devices, sum_over(): values = values + lax.ppermute(values, name, pairs)  13.5 us
    all_to_all x3, starting transfers between devices, sum_planes(): got = lax.all_to_all(rows, 'z', 0, 0, tiled=True)  12 us
    ppermute x2, waiting for transfers between devices, spread(): x_low = lax.ppermute(block[half:], 'x', SWAP)  11.9 us
  transfers between devices with their start and end apart: 56, of which 19 were waited for; matrix products, arithmetic and copies ran while one was open for 31% of the time, Pallas kernels for 0%

profile of v1, /device:TPU:0, one launch (start us, length us, event | category | flops | bytes accessed | tf_op | source)
XLA Modules:
  0.0 320.7 jit_solution(13277370663377324284)
XLA Ops:
  7.2 2.4 fusion.79
  9.6 3.0 collective-permute-start.1
  22.1 2.6 collective-permute-start.5
  27.1 3.0 collective-permute-done.3
  31.4 3.5 %all-to-all-start = ((bf16[256,4,512]{0,2,1:T(8,128)(2,1)}), bf16[256,4,512]{0,2,1:T(8,128)(2,1)S(1)}, u32[]{:S(2)}, u32[]{:S(2)}) async-start(bf16[256,4,512]{0,2,1:T(8,128)(2,1)} %bitcast.6), calls=%async_computation | async-start | bytes 2097152 | tf_op jit(solution)/shard_map/all_to_all | solution.py:138
  35.0 2.4 collective-permute-done
  54.3 2.2 collective-permute-done.8
  70.5 9.5 %collective-permute-done.11 = bf16[512,512]{1,0:T(8,128)(2,1)} collective-permute-done((bf16[512,512]{1,0:T(8,128)(2,1)}, bf16[512,512]{1,0:T(8,128)(2,1)}, u32[]{:S(2)}, u32[]{:S(2)}) %collective-permute-start.11) | collective-permute-done | bytes 524320 | tf_op jit(solution)/shard_map/ppermute | solution.py:56
  80.0 11.1 %collective-permute-done.12 = bf16[512,512]{1,0:T(8,128)(2,1)} collective-permute-done((bf16[512,512]{1,0:T(8,128)(2,1)}, bf16[512,512]{1,0:T(8,128)(2,1)}, u32[]{:S(2)}, u32[]{:S(2)}) %collective-permute-start.12) | collective-permute-done | bytes 524320 | tf_op jit(solution)/shard_map/ppermute | solution.py:57
  99.0 4.6 %collective-permute-done.15 = bf16[512,512]{1,0:T(8,128)(2,1)S(1)} collective-permute-done((bf16[512,512]{1,0:T(8,128)(2,1)}, bf16[512,512]{1,0:T(8,128)(2,1)S(1)}, u32[]{:S(2)}, u32[]{:S(2)}) %collective-permute-start.15) | collective-permute-done | bytes 524320 | tf_op jit(solution)/shard_map/ppermute | solution.py:61
  110.4 2.3 fusion.18
  117.6 2.3 fusion.28
  120.0 4.4 %all-to-all-start.1 = ((bf16[4,1,32,2048]{3,2,1,0:T(8,128)(2,1)}), bf16[4,1,32,2048]{3,2,1,0:T(8,128)(2,1)}, u32[]{:S(2)}, u32[]{:S(2)}) async-start(bf16[4,1,32,2048]{3,2,1,0:T(8,128)(2,1)} %bitcast.114), calls=%async_computation.1 | async-start | bytes 1048576 | tf_op jit(solution)/shard_map/all_to_all | solution.py:85
  124.3 5.6 %fusion.21 = f32[512,1024]{1,0:T(8,128)S(1)} fusion(bf16[256,2048]{1,0:T(8,128)(2,1)S(1)} %copy-done.5, bf16[256,2048]{1,0:T(8,128)(2,1)} %fusion.17, bf16[256,2048]{1,0:T(8,128)(2,1)} %get-tuple-element.115, bf16[256,2048]{1,0:T(8,128)(2,1)} %get-tuple-element.114, bf16[256,2048]{1,0:T(8,128)(2,1)} %get-tuple-element.113, ...), kind=kOutput, calls=%fused_computation.34 | convolution fusion | flops 2168455168 | bytes 8388608 | tf_op jit(solution)/shard_map/dot_general | solution.py:32
  132.4 7.1 %all-to-all-done.1 = bf16[4,1,32,2048]{3,2,1,0:T(8,128)(2,1)} async-done(((bf16[4,1,32,2048]{3,2,1,0:T(8,128)(2,1)}), bf16[4,1,32,2048]{3,2,1,0:T(8,128)(2,1)}, u32[]{:S(2)}, u32[]{:S(2)}) %all-to-all-start.1) | async-done | bytes 524320 | tf_op jit(solution)/shard_map/all_to_all | solution.py:85
  140.6 16.0 %all_gather.20 = bf16[128,2048]{1,0:T(8,128)(2,1)S(1)} all-gather(bf16[32,2048]{1,0:T(8,128)(2,1)S(1)} %reduce_sum.100), channel_id=1, replica_groups=mesh['z'=4,'y'=2,'x'=2,'c'=2] {'z'}, dimensions={0}, use_global_device_ids=true | all-gather | bytes 655360 | tf_op jit(solution)/shard_map/all_gather | solution.py:94
  159.6 3.0 convolution_multiply_fusion.5
  171.2 4.1 %all-to-all-start.2 = ((bf16[4,1,32,2048]{3,2,1,0:T(8,128)(2,1)}), bf16[4,1,32,2048]{3,2,1,0:T(8,128)(2,1)}, u32[]{:S(2)}, u32[]{:S(2)}) async-start(bf16[4,1,32,2048]{3,2,1,0:T(8,128)(2,1)} %bitcast.113), calls=%async_computation.2 | async-start | bytes 1048576 | tf_op jit(solution)/shard_map/all_to_all | solution.py:85
  188.3 2.3 fusion.26
  192.0 16.1 %all_gather.22 = bf16[128,2048]{1,0:T(8,128)(2,1)S(1)} all-gather(bf16[32,2048]{1,0:T(8,128)(2,1)S(1)} %reduce_sum.101), channel_id=1, replica_groups=mesh['z'=4,'y'=2,'x'=2,'c'=2] {'z'}, dimensions={0}, use_global_device_ids=true | all-gather | bytes 655360 | tf_op jit(solution)/shard_map/all_gather | solution.py:94
  229.5 5.1 %collective-permute-done.35 = bf16[512,512]{1,0:T(8,128)(2,1)S(1)} collective-permute-done((bf16[512,512]{1,0:T(8,128)(2,1)S(1)}, bf16[512,512]{1,0:T(8,128)(2,1)S(1)}, u32[]{:S(2)}, u32[]{:S(2)}) %collective-permute-start.35) | collective-permute-done | bytes 524320 | tf_op jit(solution)/shard_map/ppermute | solution.py:235
  244.9 3.0 collective-permute-done.41
  250.0 3.5 %all-to-all-start.3 = ((bf16[4,2,32,2048]{3,2,1,0:T(8,128)(2,1)}), bf16[4,2,32,2048]{3,2,1,0:T(8,128)(2,1)S(1)}, u32[]{:S(2)}, u32[]{:S(2)}) async-start(bf16[4,2,32,2048]{3,2,1,0:T(8,128)(2,1)} %pad_maximum_fusion.9), calls=%async_computation.3 | async-start | bytes 2097152 | tf_op jit(solution)/shard_map/all_to_all | solution.py:85
  253.5 4.0 %collective-permute-done.37 = bf16[512,512]{1,0:T(8,128)(2,1)S(1)} collective-permute-done((bf16[512,512]{1,0:T(8,128)(2,1)S(1)}, bf16[512,512]{1,0:T(8,128)(2,1)S(1)}, u32[]{:S(2)}, u32[]{:S(2)}) %collective-permute-start.37) | collective-permute-done | bytes 524320 | tf_op jit(solution)/shard_map/ppermute | solution.py:258
  268.5 3.6 %collective-permute-done.44 = f32[2]{0:T(128)S(1)} collective-permute-done((f32[2]{0:T(128)S(1)}, f32[2]{0:T(128)S(1)}, u32[]{:S(2)}, u32[]{:S(2)}) %collective-permute-start.44) | collective-permute-done | bytes 40 | tf_op jit(solution)/shard_map/ppermute | solution.py:46
  275.3 3.8 %all-to-all-done.3 = bf16[4,2,32,2048]{3,2,1,0:T(8,128)(2,1)S(1)} async-done(((bf16[4,2,32,2048]{3,2,1,0:T(8,128)(2,1)}), bf16[4,2,32,2048]{3,2,1,0:T(8,128)(2,1)S(1)}, u32[]{:S(2)}, u32[]{:S(2)}) %all-to-all-start.3) | async-done | bytes 1048608 | tf_op jit(solution)/shard_map/all_to_all | solution.py:85
  279.1 3.5 %all-to-all-start.4 = ((bf16[4,256,512]{2,1,0:T(8,128)(2,1)}), bf16[4,256,512]{2,1,0:T(8,128)(2,1)S(1)}, u32[]{:S(2)}, u32[]{:S(2)}) async-start(bf16[4,256,512]{2,1,0:T(8,128)(2,1)} %bitcast.39), calls=%async_computation.4 | async-start | bytes 2097152 | tf_op jit(solution)/shard_map/all_to_all | solution.py:263
  284.8 4.9 %fusion.7 = f32[256,2048]{1,0:T(8,128)S(1)} fusion(s32[2048]{0:T(1024)S(1)} %iota_multiply_fusion, s32[1024]{0:T(1024)S(1)} %add_multiply_fusion, bf16[256,256]{1,0:T(8,128)(2,1)} %collective-permute-done.47, bf16[256,256]{1,0:T(8,128)(2,1)} %collective-permute-done.46, bf16[256,256]{1,0:T(8,128)(2,1)} %collective-permute-done.45, ...), kind=kOutput, calls=%fused_computation.11 | convolution fusion | flops 1101004800 | bytes 2633728 | tf_op jit(solution)/shard_map/dot_general | solution.py:28
  289.8 3.4 %fusion.10 = f32[256,2048]{1,0:T(8,128)} fusion(f32[256,2048]{1,0:T(8,128)S(1)} %fusion.7, bf16[1024,2048]{1,0:T(8,128)(2,1)S(1)} %copy-done.53, f32[]{:T(128)} %get-tuple-element.145, f32[2048]{0:T(1024)S(1)} %copy-done.48, f32[256]{0:T(256)S(1)} %copy-done.52, f32[]{:T(128)S(6)} %mul.281, bf16[512,256]{1,0:T(8,128)(2,1)S(1)} %copy-done.44, ...), kind=kOutput, calls=%fused_computation.20 | convolution fusion | flops 1077411840 | bytes 8922120 | tf_op jit(solution)/shard_map/dot_general | solution.py:28
  293.3 14.5 %all-to-all-done.4 = bf16[4,256,512]{2,1,0:T(8,128)(2,1)S(1)} async-done(((bf16[4,256,512]{2,1,0:T(8,128)(2,1)}), bf16[4,256,512]{2,1,0:T(8,128)(2,1)S(1)}, u32[]{:S(2)}, u32[]{:S(2)}) %all-to-all-start.4) | async-done | bytes 1048608 | tf_op jit(solution)/shard_map/all_to_all | solution.py:263
  308.8 2.3 subtract_multiply_fusion
  311.1 2.2 convert_add_fusion
  (337 shorter events, 141.6 us)
Async XLA Ops:
  9.6 27.8 %collective-permute-start.1 = (bf16[128,2048]{1,0:T(8,128)(2,1)}, bf16[128,2048]{1,0:T(8,128)(2,1)}, u32[]{:S(2)}, u32[]{:S(2)}) collective-permute-start(bf16[128,2048]{1,0:T(8,128)(2,1)} %get-tuple-element.126), channel_id=1, source_target_pairs={{0,4},{4,0},{1,5},{5,1},{2,6},{6,2},{3,7},{7,3},{8,12},{12,8},{9,1... | collective-permute-start | bytes 1572872 | tf_op jit(solution)/shard_map/ppermute | solution.py:57
  12.6 28.8 %collective-permute-start.19 = (bf16[128,2048]{1,0:T(8,128)(2,1)}, bf16[128,2048]{1,0:T(8,128)(2,1)}, u32[]{:S(2)}, u32[]{:S(2)}) collective-permute-start(bf16[128,2048]{1,0:T(8,128)(2,1)} %get-tuple-element.126), channel_id=1, source_target_pairs={{0,2},{2,0},{1,3},{3,1},{4,6},{6,4},{5,7},{7,5},{8,10},{10,8},{9,1... | collective-permute-start | bytes 1572872 | tf_op jit(solution)/shard_map/ppermute | solution.py:58
  19.0 18.4 %collective-permute-start = (bf16[128,2048]{1,0:T(8,128)(2,1)}, bf16[128,2048]{1,0:T(8,128)(2,1)S(1)}, u32[]{:S(2)}, u32[]{:S(2)}) collective-permute-start(bf16[128,2048]{1,0:T(8,128)(2,1)} %get-tuple-element.127), channel_id=1, source_target_pairs={{0,2},{2,0},{1,3},{3,1},{4,6},{6,4},{5,7},{7,5},{8,10},{10,8},{9,1... | collective-permute-start | bytes 1572872 | tf_op jit(solution)/shard_map/ppermute | solution.py:56
  26.6 17.5 %collective-permute-start.18 = (bf16[128,2048]{1,0:T(8,128)(2,1)}, bf16[128,2048]{1,0:T(8,128)(2,1)}, u32[]{:S(2)}, u32[]{:S(2)}) collective-permute-start(bf16[128,2048]{1,0:T(8,128)(2,1)} %get-tuple-element.127), channel_id=1, source_target_pairs={{0,4},{4,0},{1,5},{5,1},{2,6},{6,2},{3,7},{7,3},{8,12},{12,8},{9,1... | collective-permute-start | bytes 1572872 | tf_op jit(solution)/shard_map/ppermute | solution.py:59
  31.4 31.8 %all-to-all-start = ((bf16[256,4,512]{0,2,1:T(8,128)(2,1)}), bf16[256,4,512]{0,2,1:T(8,128)(2,1)S(1)}, u32[]{:S(2)}, u32[]{:S(2)}) async-start(bf16[256,4,512]{0,2,1:T(8,128)(2,1)} %bitcast.6), calls=%async_computation | async-start | bytes 2097152 | tf_op jit(solution)/shard_map/all_to_all | solution.py:138
  35.0 68.6 %all-gather.9.cloned.1.call-start = ((), (), s32[]{:S(2)}) async-start(), calls=%async_computation.7 | async-start | bytes 1310720 | tf_op jit(solution)/shard_map/all_gather | solution.py:162
  38.2 22.8 %collective-permute-start.20 = (bf16[128,2048]{1,0:T(8,128)(2,1)}, bf16[128,2048]{1,0:T(8,128)(2,1)}, u32[]{:S(2)}, u32[]{:S(2)}) collective-permute-start(bf16[128,2048]{1,0:T(8,128)(2,1)} %collective-permute-done.1), channel_id=1, source_target_pairs={{0,2},{2,0},{1,3},{3,1},{4,6},{6,4},{5,7},{7,5},{8,10},{10,8},{9,1... | collective-permute-start | bytes 1572872 | tf_op jit(solution)/shard_map/ppermute | solution.py:61
  41.4 20.7 %collective-permute-start.21 = (bf16[128,2048]{1,0:T(8,128)(2,1)}, bf16[128,2048]{1,0:T(8,128)(2,1)}, u32[]{:S(2)}, u32[]{:S(2)}) collective-permute-start(bf16[128,2048]{1,0:T(8,128)(2,1)} %copy-done.40), channel_id=1, source_target_pairs={{0,4},{4,0},{1,5},{5,1},{2,6},{6,2},{3,7},{7,3},{8,12},{12,8},{9,1... | collective-permute-start | bytes 1572872 | tf_op jit(solution)/shard_map/ppermute | solution.py:62
  45.1 9.2 %collective-permute-start.17 = (f32[512]{0:T(512)S(1)}, f32[512]{0:T(512)S(1)}, u32[]{:S(2)}, u32[]{:S(2)}) collective-permute-start(f32[512]{0:T(512)S(1)} %dynamic_slice.87), channel_id=1, source_target_pairs={{0,2},{2,0},{1,3},{3,1},{4,6},{6,4},{5,7},{7,5},{8,10},{10,8},{9,1... | collective-permute-start | bytes 6152 | tf_op jit(solution)/shard_map/ppermute | solution.py:168
  64.8 15.1 %collective-permute-start.11 = (bf16[512,512]{1,0:T(8,128)(2,1)}, bf16[512,512]{1,0:T(8,128)(2,1)}, u32[]{:S(2)}, u32[]{:S(2)}) collective-permute-start(bf16[512,512]{1,0:T(8,128)(2,1)} %get-tuple-element.125), channel_id=1, source_target_pairs={{0,2},{2,0},{1,3},{3,1},{4,6},{6,4},{5,7},{7,5},{8,10},{10,8},{9,1... | collective-permute-start | bytes 1572872 | tf_op jit(solution)/shard_map/ppermute | solution.py:56
  66.3 28.9 %collective-permute-start.13 = (bf16[512,512]{1,0:T(8,128)(2,1)}, bf16[512,512]{1,0:T(8,128)(2,1)}, u32[]{:S(2)}, u32[]{:S(2)}) collective-permute-start(bf16[512,512]{1,0:T(8,128)(2,1)} %get-tuple-element.125), channel_id=1, source_target_pairs={{0,4},{4,0},{1,5},{5,1},{2,6},{6,2},{3,7},{7,3},{8,12},{12,8},{9,1... | collective-permute-start | bytes 1572872 | tf_op jit(solution)/shard_map/ppermute | solution.py:59
  66.8 24.2 %collective-permute-start.12 = (bf16[512,512]{1,0:T(8,128)(2,1)}, bf16[512,512]{1,0:T(8,128)(2,1)}, u32[]{:S(2)}, u32[]{:S(2)}) collective-permute-start(bf16[512,512]{1,0:T(8,128)(2,1)} %get-tuple-element.124), channel_id=1, source_target_pairs={{0,4},{4,0},{1,5},{5,1},{2,6},{6,2},{3,7},{7,3},{8,12},{12,8},{9,1... | collective-permute-start | bytes 1572872 | tf_op jit(solution)/shard_map/ppermute | solution.py:57
  68.4 24.7 %collective-permute-start.14 = (bf16[512,512]{1,0:T(8,128)(2,1)}, bf16[512,512]{1,0:T(8,128)(2,1)}, u32[]{:S(2)}, u32[]{:S(2)}) collective-permute-start(bf16[512,512]{1,0:T(8,128)(2,1)} %get-tuple-element.124), channel_id=1, source_target_pairs={{0,2},{2,0},{1,3},{3,1},{4,6},{6,4},{5,7},{7,5},{8,10},{10,8},{9,1... | collective-permute-start | bytes 1572872 | tf_op jit(solution)/shard_map/ppermute | solution.py:58
  68.9 123.0 %all-gather.5.cloned.1.call-start = ((), (), s32[]{:S(2)}) async-start(), calls=%async_computation.5 | async-start | bytes 5242880 | tf_op jit(solution)/shard_map/all_gather | solution.py:188
  91.1 12.5 %collective-permute-start.15 = (bf16[512,512]{1,0:T(8,128)(2,1)}, bf16[512,512]{1,0:T(8,128)(2,1)S(1)}, u32[]{:S(2)}, u32[]{:S(2)}) collective-permute-start(bf16[512,512]{1,0:T(8,128)(2,1)} %collective-permute-done.12), channel_id=1, source_target_pairs={{0,2},{2,0},{1,3},{3,1},{4,6},{6,4},{5,7},{7,5},{8,10},{10,8},{9,1... | collective-permute-start | bytes 1572872 | tf_op jit(solution)/shard_map/ppermute | solution.py:61
  91.7 13.3 %collective-permute-start.16 = (bf16[512,512]{1,0:T(8,128)(2,1)}, bf16[512,512]{1,0:T(8,128)(2,1)}, u32[]{:S(2)}, u32[]{:S(2)}) collective-permute-start(bf16[512,512]{1,0:T(8,128)(2,1)} %collective-permute-done.11), channel_id=1, source_target_pairs={{0,4},{4,0},{1,5},{5,1},{2,6},{6,2},{3,7},{7,3},{8,12},{12,8},{9,1... | collective-permute-start | bytes 1572872 | tf_op jit(solution)/shard_map/ppermute | solution.py:62
  120.0 19.5 %all-to-all-start.1 = ((bf16[4,1,32,2048]{3,2,1,0:T(8,128)(2,1)}), bf16[4,1,32,2048]{3,2,1,0:T(8,128)(2,1)}, u32[]{:S(2)}, u32[]{:S(2)}) async-start(bf16[4,1,32,2048]{3,2,1,0:T(8,128)(2,1)} %bitcast.114), calls=%async_computation.1 | async-start | bytes 1048576 | tf_op jit(solution)/shard_map/all_to_all | solution.py:85
  171.1 17.2 %collective-permute-start.26 = (bf16[128,2048]{1,0:T(8,128)(2,1)}, bf16[128,2048]{1,0:T(8,128)(2,1)}, u32[]{:S(2)}, u32[]{:S(2)}) collective-permute-start(bf16[128,2048]{1,0:T(8,128)(2,1)} %slice.285), channel_id=1, source_target_pairs={{0,1},{1,0},{2,3},{3,2},{4,5},{5,4},{6,7},{7,6},{8,9},{9,8},{10,11... | collective-permute-start | bytes 1572872 | tf_op jit(solution)/shard_map/ppermute | solution.py:78
  171.2 19.5 %all-to-all-start.2 = ((bf16[4,1,32,2048]{3,2,1,0:T(8,128)(2,1)}), bf16[4,1,32,2048]{3,2,1,0:T(8,128)(2,1)}, u32[]{:S(2)}, u32[]{:S(2)}) async-start(bf16[4,1,32,2048]{3,2,1,0:T(8,128)(2,1)} %bitcast.113), calls=%async_computation.2 | async-start | bytes 1048576 | tf_op jit(solution)/shard_map/all_to_all | solution.py:85
  219.8 14.8 %collective-permute-start.35 = (bf16[512,512]{1,0:T(8,128)(2,1)S(1)}, bf16[512,512]{1,0:T(8,128)(2,1)S(1)}, u32[]{:S(2)}, u32[]{:S(2)}) collective-permute-start(bf16[512,512]{1,0:T(8,128)(2,1)S(1)} %convolution_convert_fusion.3), channel_id=1, source_target_pairs={{0,2},{2,0},{1,3},{3,1},{4,6},{6,4},{5,7},{7,5},{8,10},{10,8},{9,1... | collective-permute-start | bytes 1572872 | tf_op jit(solution)/shard_map/ppermute | solution.py:235
  221.1 14.8 %collective-permute-start.36 = (bf16[512,512]{1,0:T(8,128)(2,1)S(1)}, bf16[512,512]{1,0:T(8,128)(2,1)S(1)}, u32[]{:S(2)}, u32[]{:S(2)}) collective-permute-start(bf16[512,512]{1,0:T(8,128)(2,1)S(1)} %convolution_convert_fusion.2), channel_id=1, source_target_pairs={{0,4},{4,0},{1,5},{5,1},{2,6},{6,2},{3,7},{7,3},{8,12},{12,8},{9,1... | collective-permute-start | bytes 1572872 | tf_op jit(solution)/shard_map/ppermute | solution.py:236
  223.8 29.8 %collective-permute-start.34 = (bf16[512,512]{1,0:T(8,128)(2,1)}, bf16[512,512]{1,0:T(8,128)(2,1)}, u32[]{:S(2)}, u32[]{:S(2)}) collective-permute-start(bf16[512,512]{1,0:T(8,128)(2,1)} %convolution_convert_fusion.1), channel_id=1, source_target_pairs={{0,2},{2,0},{1,3},{3,1},{4,6},{6,4},{5,7},{7,5},{8,10},{10,8},{9,1... | collective-permute-start | bytes 1572872 | tf_op jit(solution)/shard_map/ppermute | solution.py:237
  225.6 33.1 %collective-permute-start.39 = (bf16[512,512]{1,0:T(8,128)(2,1)}, bf16[512,512]{1,0:T(8,128)(2,1)}, u32[]{:S(2)}, u32[]{:S(2)}) collective-permute-start(bf16[512,512]{1,0:T(8,128)(2,1)} %convolution_convert_fusion), channel_id=1, source_target_pairs={{0,4},{4,0},{1,5},{5,1},{2,6},{6,2},{3,7},{7,3},{8,12},{12,8},{9,1... | collective-permute-start | bytes 1572872 | tf_op jit(solution)/shard_map/ppermute | solution.py:238
  226.5 17.7 %collective-permute-start.33 = (bf16[128,2048]{1,0:T(8,128)(2,1)S(1)}, bf16[128,2048]{1,0:T(8,128)(2,1)S(1)}, u32[]{:S(2)}, u32[]{:S(2)}) collective-permute-start(bf16[128,2048]{1,0:T(8,128)(2,1)S(1)} %slice.284), channel_id=1, source_target_pairs={{0,1},{1,0},{2,3},{3,2},{4,5},{5,4},{6,7},{7,6},{8,9},{9,8},{10,11... | collective-permute-start | bytes 1572872 | tf_op jit(solution)/shard_map/ppermute | solution.py:78
  239.5 18.0 %collective-permute-start.37 = (bf16[512,512]{1,0:T(8,128)(2,1)S(1)}, bf16[512,512]{1,0:T(8,128)(2,1)S(1)}, u32[]{:S(2)}, u32[]{:S(2)}) collective-permute-start(bf16[512,512]{1,0:T(8,128)(2,1)S(1)} %add_convert_fusion.4), channel_id=1, source_target_pairs={{0,4},{4,0},{1,5},{5,1},{2,6},{6,2},{3,7},{7,3},{8,12},{12,8},{9,1... | collective-permute-start | bytes 1572872 | tf_op jit(solution)/shard_map/ppermute | solution.py:258
  242.3 16.5 %collective-permute-start.38 = (bf16[512,512]{1,0:T(8,128)(2,1)}, bf16[512,512]{1,0:T(8,128)(2,1)}, u32[]{:S(2)}, u32[]{:S(2)}) collective-permute-start(bf16[512,512]{1,0:T(8,128)(2,1)} %add_convert_fusion.2), channel_id=1, source_target_pairs={{0,2},{2,0},{1,3},{3,1},{4,6},{6,4},{5,7},{7,5},{8,10},{10,8},{9,1... | collective-permute-start | bytes 1572872 | tf_op jit(solution)/shard_map/ppermute | solution.py:257
  250.0 29.1 %all-to-all-start.3 = ((bf16[4,2,32,2048]{3,2,1,0:T(8,128)(2,1)}), bf16[4,2,32,2048]{3,2,1,0:T(8,128)(2,1)S(1)}, u32[]{:S(2)}, u32[]{:S(2)}) async-start(bf16[4,2,32,2048]{3,2,1,0:T(8,128)(2,1)} %pad_maximum_fusion.9), calls=%async_computation.3 | async-start | bytes 2097152 | tf_op jit(solution)/shard_map/all_to_all | solution.py:85
  263.1 21.7 %collective-permute-start.45 = (bf16[256,256]{1,0:T(8,128)(2,1)}, bf16[256,256]{1,0:T(8,128)(2,1)}, u32[]{:S(2)}, u32[]{:S(2)}) collective-permute-start(bf16[256,256]{1,0:T(8,128)(2,1)} %get-tuple-element.133), channel_id=1, source_target_pairs={{0,2},{2,0},{1,3},{3,1},{4,6},{6,4},{5,7},{7,5},{8,10},{10,8},{9,1... | collective-permute-start | bytes 393224 | tf_op jit(solution)/shard_map/ppermute | solution.py:70
  264.3 20.5 %collective-permute-start.46 = (bf16[256,256]{1,0:T(8,128)(2,1)S(1)}, bf16[256,256]{1,0:T(8,128)(2,1)}, u32[]{:S(2)}, u32[]{:S(2)}) collective-permute-start(bf16[256,256]{1,0:T(8,128)(2,1)S(1)} %get-tuple-element.132), channel_id=1, source_target_pairs={{0,4},{4,0},{1,5},{5,1},{2,6},{6,2},{3,7},{7,3},{8,12},{12,8},{9,1... | collective-permute-start | bytes 393224 | tf_op jit(solution)/shard_map/ppermute | solution.py:71
  265.7 19.1 %collective-permute-start.47 = (bf16[256,256]{1,0:T(8,128)(2,1)S(1)}, bf16[256,256]{1,0:T(8,128)(2,1)}, u32[]{:S(2)}, u32[]{:S(2)}) collective-permute-start(bf16[256,256]{1,0:T(8,128)(2,1)S(1)} %get-tuple-element.131), channel_id=1, source_target_pairs={{0,6},{2,4},{4,2},{6,0},{1,7},{3,5},{5,3},{7,1},{8,14},{10,12},{12... | collective-permute-start | bytes 393224 | tf_op jit(solution)/shard_map/ppermute | solution.py:72
  279.1 28.7 %all-to-all-start.4 = ((bf16[4,256,512]{2,1,0:T(8,128)(2,1)}), bf16[4,256,512]{2,1,0:T(8,128)(2,1)S(1)}, u32[]{:S(2)}, u32[]{:S(2)}) async-start(bf16[4,256,512]{2,1,0:T(8,128)(2,1)} %bitcast.39), calls=%async_computation.4 | async-start | bytes 2097152 | tf_op jit(solution)/shard_map/all_to_all | solution.py:263
  282.6 28.5 %all-gather.7.cloned.1.call-start = ((), (), s32[]{:S(2)}) async-start(), calls=%async_computation.6 | async-start | bytes 1310720 | tf_op jit(solution)/shard_map/all_gather | solution.py:253
  (79 other events, 388.2 us)
Sparse Core Ops, SparseCore 0:
  69.0 28.2 all-gather.8
  120.1 52.2 all-gather.4
  285.6 17.4 all-gather.6

commit v2 on v1

--- a/solution.py
+++ b/solution.py
@@ -79,11 +79,10 @@
     return (part[:half] + got.astype(F32)).astype(BF16)
 
 
-def sum_planes(*parts):
+def sum_planes(rows):
     planes = lax.axis_size("z")
-    rows = jnp.stack([part.reshape(planes, -1, part.shape[1]) for part in parts], 1)
     got = lax.all_to_all(rows, "z", 0, 0, tiled=True)
-    return jnp.sum(got.astype(F32), 0)
+    return jnp.sum(got.reshape(planes, rows.shape[0] // planes, -1).astype(F32), 0)
 
 
 def with_other_core(half):
@@ -147,10 +146,10 @@
 
     tok_own = own_quarter(tokens)
     in_z, pair = tied((in_z, jnp.stack([tok_own, own_quarter(cotangent)])))
-    (in_x, in_y, in_d), _ = spread(in_z)
-    full_in = jnp.concatenate([join_rows(in_z, in_y), join_rows(in_x, in_d)], 1)
-
     sums = sum_over(sums, ("y",))
+    seeds = with_other_core(seeds)
+    (in_x, in_y, in_d), (sums, bias_own) = spread(in_z, sums, bias_own)
+
     p_vec = sums[:hid_rep]
     sums = sum_over(jnp.concatenate([sums[hid_rep:], jnp.sum(p_vec * p_vec)[None]]), ("c", "x"))
     q_vec = sums[:width]
@@ -163,9 +162,10 @@
     tok = with_other_core(pair[0].reshape(-1, width))
     cot = with_other_core(pair[1].reshape(-1, width))
     n = tok.shape[0]
-    seeds = with_other_core(seeds)
     probe = probe_signs(seeds, width)
     bias_all = jnp.concatenate([bias_own, lax.ppermute(bias_own, "x", SWAP)])
+    in_d, tok, cot, probe = tied((in_d, tok, cot, probe))
+    full_in = jnp.concatenate([join_rows(in_z, in_y), join_rows(in_x, in_d)], 1)
 
     raw = times(jnp.concatenate([tok, probe], 0), full_in)
     raw_z = raw[:n]
@@ -196,7 +196,7 @@
     raw_c = backs[n:]
     hd = deriv * (scale_out * raw_b)
     h_round = hd.astype(BF16)
-    quarter_one = sum_planes(j_pair)[0].astype(BF16)
+    quarter_one = sum_planes(j_pair).astype(BF16)
     quarter_one, h_round, raw_c = tied((quarter_one, h_round, raw_c))
     j_one = gather_rows(quarter_one)
 
@@ -205,7 +205,7 @@
     j_pair = fold_cores(scale_out * times(r_two, full_out))
     j_pair, act_late = tied((j_pair, act_late))
     branch = fold_cores(scale_out * times(act_late, full_out))
-    quarter_two = sum_planes(j_pair)[0].astype(BF16)
+    quarter_two = sum_planes(j_pair).astype(BF16)
     if factors:
         quarter_two, branch, seeds_all, cot_rows, act_units = tied(
             (quarter_two, branch, seeds_all, cot_rows, act_units)
@@ -231,35 +231,40 @@
     over_top, over_low = over[:, :half], over[:, half:]
     across_x = contract_rows(over_top, other_cols).astype(BF16)
     across_y = contract_rows(over_low, other_cols).astype(BF16)
-    across_x, across_y, own_cols, other_cols = tied((across_x, across_y, own_cols, other_cols))
+    across_x, across_y, g_late, a_late, e_late, dz_late = tied(
+        (across_x, across_y, g_round, a_vec, e_three, dz_round)
+    )
     across_x = lax.ppermute(across_x, "x", SWAP)
     across_y = lax.ppermute(across_y, "y", SWAP)
-    x_top = lax.ppermute(contract_rows(near_top, other_cols).astype(BF16), "x", SWAP)
-    y_low = lax.ppermute(contract_rows(over_low, own_cols).astype(BF16), "y", SWAP)
-    dx = fold_cores(scale_in * contract_cols(dz_round, full_in))
-    ends = sum_planes(branch, dx)
-    ends = jnp.stack([tok_own.astype(F32) + ends[0], ends[1]]).astype(BF16)
-    across_x, across_y, g_late, a_late, e_late, dz_late = tied(
-        (across_x, across_y, g_round, a_vec, e_three, dz_round)
-    )
+    dx = fold_cores(scale_in * contract_cols(dz_late, full_in))
     terms = jnp.sum((e_one - e_two / 2.0 + e_late / 3.0) * hd, axis=1)
     inner_one = jnp.sum(dz_late.astype(F32) * raw_z - h_round.astype(F32) * (a_late / scale_in))
     inner_two = jnp.sum(act.astype(F32) * raw_c - g_late.astype(F32) * raw_b)
     inner = jnp.stack([inner_one, inner_two])
     tail = jnp.concatenate([terms, inner])
     got = lax.ppermute(tail, "c", SWAP)
-    got = jnp.concatenate([got[n // 2 : n], got[: n // 2], got[n:]])
-    tail = sum_over(tail + got, ("z",))
-    ends = lax.all_gather(ends, ("x", "c"), axis=1, tiled=True)
-
+    tail = tail + jnp.concatenate([got[n // 2 : n], got[: n // 2], got[n:]])
+    across_x, across_y, own_cols, other_cols, dx, tail = tied(
+        (across_x, across_y, own_cols, other_cols, dx, tail)
+    )
+    x_top = lax.ppermute(contract_rows(near_top, other_cols).astype(BF16), "x", SWAP)
+    y_low = lax.ppermute(contract_rows(over_low, own_cols).astype(BF16), "y", SWAP)
     x_low = contract_rows(near_low, other_cols) + across_y.astype(F32)
     y_top = contract_rows(over_top, own_cols) + across_x.astype(F32)
     x_low = lax.ppermute(x_low.astype(BF16), "x", SWAP)
     y_top = lax.ppermute(y_top.astype(BF16), "y", SWAP)
+    ends = jnp.stack([rows.reshape(planes, quarter, width) for rows in (branch, dx)], 1)
+    ends = lax.psum_scatter(ends, "z", scatter_dimension=0, tiled=True)[0].astype(F32)
+    ends = jnp.stack([tok_own.astype(F32) + ends[0], ends[1]]).astype(BF16)
+    ends = lax.all_gather(ends, ("x", "c"), axis=1, tiled=True)
+    tail = sum_over(tail, ("z",))
     top = contract_rows(near_top, own_cols) + x_top.astype(F32) + y_top.astype(F32)
     low = contract_rows(near_low, own_cols) + x_low.astype(F32) + y_low.astype(F32)
     block = jnp.concatenate([top.astype(BF16), low.astype(BF16)], 0)
-    block, tail, g_late = tied((block, tail, g_late))
+    if factors:
+        block, tail, g_late, act_units = tied((block, tail, g_late, act_units))
+    else:
+        block, tail, g_late = tied((block, tail, g_late))
     grad_one = lax.all_to_all(block, "z", 0, 1, tiled=True).astype(F32)
 
     if factors:

time: 322 us -> 315 us (0.978)
  local copies, waits for them, and re-layouts: 38.6 us -> 32.4 us
  waiting for transfers between devices: 81.2 us -> 84.5 us
    all_to_all x1, waiting for transfers between devices: 14.5 us -> 4.19 us  [on_device(): grad_one = lax.all_to_all(block, 'z', 0, 1, tiled=True).astype(F32)]
    ppermute x2, waiting for transfers between devices: 11.1 us -> 2.37 us  [spread(): y_top = lax.ppermute(block[:half], 'y', SWAP)]
    ppermute x2, waiting for transfers between devices: 11.9 us -> 18.4 us  [spread(): x_low = lax.ppermute(block[half:], 'x', SWAP)]
    ppermute x1, waiting for transfers between devices: 0.01 us -> 5.7 us  [on_device(): x_low = lax.ppermute(x_low.astype(BF16), 'x', SWAP)]
    ppermute x1, waiting for transfers between devices: 5.14 us -> 9.97 us  [on_device(): across_x = lax.ppermute(across_x, 'x', SWAP)]
    all_to_all x1, waiting for transfers between devices: 0.01 us -> 4.05 us  [on_device(): in_z = lax.all_to_all(w_late, 'z', 1, 0, tiled=True)]
    concatenate x2 -> x3, other arithmetic: 1.14 us -> 4.94 us  [with_other_core(): return jnp.concatenate([half, lax.ppermute(half, 'c', SWAP)], 0)]
    all_to_all x3 -> x2, starting transfers between devices: 12 us -> 8.28 us  [sum_planes(): got = lax.all_to_all(rows, 'z', 0, 0, tiled=True)]
  transfers between devices with their start and end apart: 56 -> 56, of which waited for: 19 -> 25; matrix products, arithmetic and copies ran while one was open for 31% -> 29% of each run, Pallas kernels for 0% -> 0%
where the time goes in v2:
time: 315 us; the launch traced here: 313 us
  waiting for transfers between devices  84.5 us (27%)
  starting transfers between devices  59.2 us (19%)
  other arithmetic  51.9 us (16%)
  matrix products  35.8 us (11%)
  local copies, waits for them, and re-layouts  32.4 us (10%)
  blocking collectives  32.2 us (10%)
  between operations  17.4 us (6%)
    all_gather x2, blocking collectives, gather_rows(): return with_other_core(lax.all_gather(quarter, 'z', axis=0, tiled=True))  32.2 us
    ppermute x2, waiting for transfers between devices, spread(): x_low = lax.ppermute(block[half:], 'x', SWAP)  18.4 us
    dot_general x10, matrix products, contract_rows(): lax.dot_general(left, right, (((0,), (0,)), ((), ())), preferred_element_...  16.1 us
    ppermute x12, starting transfers between devices, sum_over(): values = values + lax.ppermute(values, name, pairs)  13.9 us
    unnamed x102, local copies, waits for them, and re-layouts  13.8 us
    dot_general x8, matrix products, times(): return jnp.dot(left, right, preferred_element_type=F32)  11.8 us
    ppermute x12, waiting for transfers between devices, sum_over(): values = values + lax.ppermute(values, name, pairs)  10.6 us
    ppermute x1, waiting for transfers between devices, on_device(): across_x = lax.ppermute(across_x, 'x', SWAP)  9.97 us
  transfers between devices with their start and end apart: 56, of which 25 were waited for; matrix products, arithmetic and copies ran while one was open for 29% of the time, Pallas kernels for 0%

profile of v2, /device:TPU:0, one launch (start us, length us, event | category | flops | bytes accessed | tf_op | source)
XLA Modules:
  0.0 313.4 jit_solution(11534965568005583354)
XLA Ops:
  7.2 2.4 fusion.86
  9.6 2.9 collective-permute-start.6
  22.1 2.6 collective-permute-start.3
  27.1 3.0 collective-permute-done.1
  31.4 3.5 %all-to-all-start = ((bf16[256,4,512]{0,2,1:T(8,128)(2,1)}), bf16[256,4,512]{0,2,1:T(8,128)(2,1)S(1)}, u32[]{:S(2)}, u32[]{:S(2)}) async-start(bf16[256,4,512]{0,2,1:T(8,128)(2,1)} %bitcast.3), calls=%async_computation | async-start | bytes 2097152 | tf_op jit(solution)/shard_map/all_to_all | solution.py:137
  35.0 2.4 collective-permute-done.7
  47.1 6.2 %collective-permute-done.21 = bf16[128,2048]{1,0:T(8,128)(2,1)S(1)} collective-permute-done((bf16[128,2048]{1,0:T(8,128)(2,1)S(1)}, bf16[128,2048]{1,0:T(8,128)(2,1)S(1)}, u32[]{:S(2)}, u32[]{:S(2)}) %collective-permute-start.21) | collective-permute-done | bytes 524320 | tf_op jit(solution)/shard_map/ppermute | solution.py:61
  53.9 4.0 %all-to-all-done = bf16[256,4,512]{0,2,1:T(8,128)(2,1)S(1)} async-done(((bf16[256,4,512]{0,2,1:T(8,128)(2,1)}), bf16[256,4,512]{0,2,1:T(8,128)(2,1)S(1)}, u32[]{:S(2)}, u32[]{:S(2)}) %all-to-all-start) | async-done | bytes 1048608 | tf_op jit(solution)/shard_map/all_to_all | solution.py:137
  62.9 2.7 broadcast_select_fusion.1
  66.2 18.4 %collective-permute-done.4 = bf16[512,512]{1,0:T(8,128)(2,1)} collective-permute-done((bf16[512,512]{1,0:T(8,128)(2,1)}, bf16[512,512]{1,0:T(8,128)(2,1)}, u32[]{:S(2)}, u32[]{:S(2)}) %collective-permute-start.4) | collective-permute-done | bytes 524320 | tf_op jit(solution)/shard_map/ppermute | solution.py:56
  106.2 2.3 pad_maximum_fusion.8
  111.3 2.3 fusion.18
  118.1 4.2 %all-to-all-start.1 = ((bf16[4,32,2048]{2,1,0:T(8,128)(2,1)}), bf16[4,32,2048]{2,1,0:T(8,128)(2,1)}, u32[]{:S(2)}, u32[]{:S(2)}) async-start(bf16[4,32,2048]{2,1,0:T(8,128)(2,1)} %bitcast.109), calls=%async_computation.1 | async-start | bytes 1048576 | tf_op jit(solution)/shard_map/all_to_all | solution.py:84
  122.3 6.4 %fusion.20 = f32[512,1024]{1,0:T(8,128)S(1)} fusion(bf16[256,2048]{1,0:T(8,128)(2,1)} %pad_maximum_fusion.8, bf16[256,2048]{1,0:T(8,128)(2,1)} %fusion.17, bf16[256,2048]{1,0:T(8,128)(2,1)} %get-tuple-element.139, bf16[256,2048]{1,0:T(8,128)(2,1)} %get-tuple-element.138, bf16[256,2048]{1,0:T(8,128)(2,1)} %get-tuple-element.137, ...), kind=kOutput, calls=%fused_computation.49 | convolution fusion | flops 2168455168 | bytes 8388608 | tf_op jit(solution)/shard_map/dot_general | solution.py:32
  131.4 6.3 %all-to-all-done.1 = bf16[4,32,2048]{2,1,0:T(8,128)(2,1)} async-done(((bf16[4,32,2048]{2,1,0:T(8,128)(2,1)}), bf16[4,32,2048]{2,1,0:T(8,128)(2,1)}, u32[]{:S(2)}, u32[]{:S(2)}) %all-to-all-start.1) | async-done | bytes 524320 | tf_op jit(solution)/shard_map/all_to_all | solution.py:84
  138.8 15.9 %all_gather.20 = bf16[128,2048]{1,0:T(8,128)(2,1)S(1)} all-gather(bf16[32,2048]{1,0:T(8,128)(2,1)S(1)} %reduce_sum.91), channel_id=1, replica_groups=mesh['z'=4,'y'=2,'x'=2,'c'=2] {'z'}, dimensions={0}, use_global_device_ids=true | all-gather | bytes 655360 | tf_op jit(solution)/shard_map/all_gather | solution.py:93
  157.6 3.0 convolution_multiply_fusion.5
  169.3 4.1 %all-to-all-start.2 = ((bf16[4,32,2048]{2,1,0:T(8,128)(2,1)}), bf16[4,32,2048]{2,1,0:T(8,128)(2,1)}, u32[]{:S(2)}, u32[]{:S(2)}) async-start(bf16[4,32,2048]{2,1,0:T(8,128)(2,1)} %bitcast.108), calls=%async_computation.2 | async-start | bytes 1048576 | tf_op jit(solution)/shard_map/all_to_all | solution.py:84
  174.3 2.9 collective-permute-done.27
  181.8 2.4 collective-permute-start.31
  186.5 2.3 all-to-all-done.2
  190.0 16.4 %all_gather.22 = bf16[128,2048]{1,0:T(8,128)(2,1)} all-gather(bf16[32,2048]{1,0:T(8,128)(2,1)S(1)} %reduce_sum.92), channel_id=1, replica_groups=mesh['z'=4,'y'=2,'x'=2,'c'=2] {'z'}, dimensions={0}, use_global_device_ids=true | all-gather | bytes 655360 | tf_op jit(solution)/shard_map/all_gather | solution.py:93
  225.4 10.0 %collective-permute-done.33 = bf16[512,512]{1,0:T(8,128)(2,1)S(1)} collective-permute-done((bf16[512,512]{1,0:T(8,128)(2,1)S(1)}, bf16[512,512]{1,0:T(8,128)(2,1)S(1)}, u32[]{:S(2)}, u32[]{:S(2)}) %collective-permute-start.33) | collective-permute-done | bytes 524320 | tf_op jit(solution)/shard_map/ppermute | solution.py:237
  246.7 2.5 collective-permute-start.42
  251.2 2.8 collective-permute-done.37
  257.2 5.7 %collective-permute-done.39 = bf16[512,512]{1,0:T(8,128)(2,1)S(1)} collective-permute-done((bf16[512,512]{1,0:T(8,128)(2,1)}, bf16[512,512]{1,0:T(8,128)(2,1)S(1)}, u32[]{:S(2)}, u32[]{:S(2)}) %collective-permute-start.39) | collective-permute-done | bytes 524320 | tf_op jit(solution)/shard_map/ppermute | solution.py:254
  272.4 3.9 %all-to-all-start.3 = ((bf16[4,256,512]{2,1,0:T(8,128)(2,1)}), bf16[4,256,512]{2,1,0:T(8,128)(2,1)S(1)}, u32[]{:S(2)}, u32[]{:S(2)}) async-start(bf16[4,256,512]{2,1,0:T(8,128)(2,1)} %bitcast.38), calls=%async_computation.4 | async-start | bytes 2097152 | tf_op jit(solution)/shard_map/all_to_all | solution.py:268
  279.3 2.5 collective-permute-done.44
  287.3 3.8 %fusion.7 = f32[256,2048]{1,0:T(8,128)S(1)} fusion(s32[2048]{0:T(1024)S(1)} %iota_multiply_fusion, s32[1024]{0:T(1024)S(1)} %add_multiply_fusion, bf16[256,256]{1,0:T(8,128)(2,1)S(1)} %collective-permute-done.47, bf16[256,256]{1,0:T(8,128)(2,1)S(1)} %collective-permute-done.46, bf16[256,256]{1,0:T(8,128)(2,1)S(1)} %collective-permute-done.45, ...), kind=kOutput, calls=%fused_computation.20 | convolution fusion | flops 1101004800 | bytes 2633728 | tf_op jit(solution)/shard_map/dot_general | solution.py:28
  291.1 3.3 %fusion.10 = f32[256,2048]{1,0:T(8,128)} fusion(f32[256,2048]{1,0:T(8,128)S(1)} %fusion.7, bf16[1024,2048]{1,0:T(8,128)(2,1)S(1)} %copy-done.45, f32[]{:T(128)} %get-tuple-element.169, f32[2048]{0:T(1024)S(1)} %copy-done.41, f32[256]{0:T(256)S(1)} %convert_multiply_fusion, f32[]{:T(128)S(6)} %mul.281, bf16[512,256]{1,0:T(8,128)(2,1)S(1)} %get-tuple-element.153, ...), kind=kOutput, calls=%fused_computation.37 | convolution fusion | flops 1077411840 | bytes 8922120 | tf_op jit(solution)/shard_map/dot_general | solution.py:28
  294.4 4.2 %all-to-all-done.3 = bf16[4,256,512]{2,1,0:T(8,128)(2,1)S(1)} async-done(((bf16[4,256,512]{2,1,0:T(8,128)(2,1)}), bf16[4,256,512]{2,1,0:T(8,128)(2,1)S(1)}, u32[]{:S(2)}, u32[]{:S(2)}) %all-to-all-start.3) | async-done | bytes 1048608 | tf_op jit(solution)/shard_map/all_to_all | solution.py:268
  299.6 2.4 subtract_multiply_fusion
  (319 shorter events, 138.5 us)
Async XLA Ops:
  9.6 25.4 %collective-permute-start.6 = (bf16[128,2048]{1,0:T(8,128)(2,1)}, bf16[128,2048]{1,0:T(8,128)(2,1)}, u32[]{:S(2)}, u32[]{:S(2)}) collective-permute-start(bf16[128,2048]{1,0:T(8,128)(2,1)} %get-tuple-element.149), channel_id=1, source_target_pairs={{0,2},{2,0},{1,3},{3,1},{4,6},{6,4},{5,7},{7,5},{8,10},{10,8},{9,1... | collective-permute-start | bytes 1572872 | tf_op jit(solution)/shard_map/ppermute | solution.py:56
  12.6 26.9 %collective-permute-start.19 = (bf16[128,2048]{1,0:T(8,128)(2,1)}, bf16[128,2048]{1,0:T(8,128)(2,1)S(1)}, u32[]{:S(2)}, u32[]{:S(2)}) collective-permute-start(bf16[128,2048]{1,0:T(8,128)(2,1)} %get-tuple-element.149), channel_id=1, source_target_pairs={{0,4},{4,0},{1,5},{5,1},{2,6},{6,2},{3,7},{7,3},{8,12},{12,8},{9,1... | collective-permute-start | bytes 1572872 | tf_op jit(solution)/shard_map/ppermute | solution.py:59
  19.0 18.3 %collective-permute-start.7 = (bf16[128,2048]{1,0:T(8,128)(2,1)}, bf16[128,2048]{1,0:T(8,128)(2,1)S(1)}, u32[]{:S(2)}, u32[]{:S(2)}) collective-permute-start(bf16[128,2048]{1,0:T(8,128)(2,1)} %get-tuple-element.148), channel_id=1, source_target_pairs={{0,4},{4,0},{1,5},{5,1},{2,6},{6,2},{3,7},{7,3},{8,12},{12,8},{9,1... | collective-permute-start | bytes 1572872 | tf_op jit(solution)/shard_map/ppermute | solution.py:57
  26.6 14.9 %collective-permute-start.20 = (bf16[128,2048]{1,0:T(8,128)(2,1)}, bf16[128,2048]{1,0:T(8,128)(2,1)}, u32[]{:S(2)}, u32[]{:S(2)}) collective-permute-start(bf16[128,2048]{1,0:T(8,128)(2,1)} %get-tuple-element.148), channel_id=1, source_target_pairs={{0,2},{2,0},{1,3},{3,1},{4,6},{6,4},{5,7},{7,5},{8,10},{10,8},{9,1... | collective-permute-start | bytes 1572872 | tf_op jit(solution)/shard_map/ppermute | solution.py:58
  31.4 26.5 %all-to-all-start = ((bf16[256,4,512]{0,2,1:T(8,128)(2,1)}), bf16[256,4,512]{0,2,1:T(8,128)(2,1)S(1)}, u32[]{:S(2)}, u32[]{:S(2)}) async-start(bf16[256,4,512]{0,2,1:T(8,128)(2,1)} %bitcast.3), calls=%async_computation | async-start | bytes 2097152 | tf_op jit(solution)/shard_map/all_to_all | solution.py:137
  35.0 60.2 %all-gather.9.cloned.1.call-start = ((), (), s32[]{:S(2)}) async-start(), calls=%async_computation.8 | async-start | bytes 1310720 | tf_op jit(solution)/shard_map/all_gather | solution.py:161
  37.4 9.7 %collective-permute-start.8 = (f32[4097]{0:T(1024)S(1)}, f32[4097]{0:T(1024)S(1)}, u32[]{:S(2)}, u32[]{:S(2)}) collective-permute-start(f32[4097]{0:T(1024)S(1)} %add.232), channel_id=1, source_target_pairs={{0,4},{4,0},{1,5},{5,1},{2,6},{6,2},{3,7},{7,3},{8,12},{12,8},{9,1... | collective-permute-start | bytes 49172 | tf_op jit(solution)/shard_map/ppermute | solution.py:46
  38.9 14.3 %collective-permute-start.21 = (bf16[128,2048]{1,0:T(8,128)(2,1)S(1)}, bf16[128,2048]{1,0:T(8,128)(2,1)S(1)}, u32[]{:S(2)}, u32[]{:S(2)}) collective-permute-start(bf16[128,2048]{1,0:T(8,128)(2,1)S(1)} %collective-permute-done.7), channel_id=1, source_target_pairs={{0,2},{2,0},{1,3},{3,1},{4,6},{6,4},{5,7},{7,5},{8,10},{10,8},{9,1... | collective-permute-start | bytes 1572872 | tf_op jit(solution)/shard_map/ppermute | solution.py:61
  39.5 14.3 %collective-permute-start.22 = (bf16[128,2048]{1,0:T(8,128)(2,1)}, bf16[128,2048]{1,0:T(8,128)(2,1)S(1)}, u32[]{:S(2)}, u32[]{:S(2)}) collective-permute-start(bf16[128,2048]{1,0:T(8,128)(2,1)} %collective-permute-done.6), channel_id=1, source_target_pairs={{0,4},{4,0},{1,5},{5,1},{2,6},{6,2},{3,7},{7,3},{8,12},{12,8},{9,1... | collective-permute-start | bytes 1572872 | tf_op jit(solution)/shard_map/ppermute | solution.py:62
  59.3 25.3 %collective-permute-start.5 = (bf16[512,512]{1,0:T(8,128)(2,1)S(1)}, bf16[512,512]{1,0:T(8,128)(2,1)}, u32[]{:S(2)}, u32[]{:S(2)}) collective-permute-start(bf16[512,512]{1,0:T(8,128)(2,1)S(1)} %get-tuple-element.150), channel_id=1, source_target_pairs={{0,4},{4,0},{1,5},{5,1},{2,6},{6,2},{3,7},{7,3},{8,12},{12,8},{9,1... | collective-permute-start | bytes 1572872 | tf_op jit(solution)/shard_map/ppermute | solution.py:57
  60.8 27.7 %collective-permute-start.17 = (bf16[512,512]{1,0:T(8,128)(2,1)S(1)}, bf16[512,512]{1,0:T(8,128)(2,1)}, u32[]{:S(2)}, u32[]{:S(2)}) collective-permute-start(bf16[512,512]{1,0:T(8,128)(2,1)S(1)} %get-tuple-element.150), channel_id=1, source_target_pairs={{0,2},{2,0},{1,3},{3,1},{4,6},{6,4},{5,7},{7,5},{8,10},{10,8},{9,1... | collective-permute-start | bytes 1572872 | tf_op jit(solution)/shard_map/ppermute | solution.py:58
  61.3 23.2 %collective-permute-start.4 = (bf16[512,512]{1,0:T(8,128)(2,1)}, bf16[512,512]{1,0:T(8,128)(2,1)}, u32[]{:S(2)}, u32[]{:S(2)}) collective-permute-start(bf16[512,512]{1,0:T(8,128)(2,1)} %get-tuple-element.151), channel_id=1, source_target_pairs={{0,2},{2,0},{1,3},{3,1},{4,6},{6,4},{5,7},{7,5},{8,10},{10,8},{9,1... | collective-permute-start | bytes 1572872 | tf_op jit(solution)/shard_map/ppermute | solution.py:56
  62.8 127.1 %all-gather.5.cloned.1.call-start = ((), (), s32[]{:S(2)}) async-start(), calls=%async_computation.5 | async-start | bytes 5242880 | tf_op jit(solution)/shard_map/all_gather | solution.py:188
  65.6 23.9 %collective-permute-start.16 = (bf16[512,512]{1,0:T(8,128)(2,1)}, bf16[512,512]{1,0:T(8,128)(2,1)S(1)}, u32[]{:S(2)}, u32[]{:S(2)}) collective-permute-start(bf16[512,512]{1,0:T(8,128)(2,1)} %get-tuple-element.151), channel_id=1, source_target_pairs={{0,4},{4,0},{1,5},{5,1},{2,6},{6,2},{3,7},{7,3},{8,12},{12,8},{9,1... | collective-permute-start | bytes 1572872 | tf_op jit(solution)/shard_map/ppermute | solution.py:59
  84.6 18.3 %collective-permute-start.11 = (bf16[512,512]{1,0:T(8,128)(2,1)}, bf16[512,512]{1,0:T(8,128)(2,1)S(1)}, u32[]{:S(2)}, u32[]{:S(2)}) collective-permute-start(bf16[512,512]{1,0:T(8,128)(2,1)} %collective-permute-done.5), channel_id=1, source_target_pairs={{0,2},{2,0},{1,3},{3,1},{4,6},{6,4},{5,7},{7,5},{8,10},{10,8},{9,1... | collective-permute-start | bytes 1572872 | tf_op jit(solution)/shard_map/ppermute | solution.py:61
  85.1 18.5 %collective-permute-start.12 = (bf16[512,512]{1,0:T(8,128)(2,1)}, bf16[512,512]{1,0:T(8,128)(2,1)}, u32[]{:S(2)}, u32[]{:S(2)}) collective-permute-start(bf16[512,512]{1,0:T(8,128)(2,1)} %collective-permute-done.4), channel_id=1, source_target_pairs={{0,4},{4,0},{1,5},{5,1},{2,6},{6,2},{3,7},{7,3},{8,12},{12,8},{9,1... | collective-permute-start | bytes 1572872 | tf_op jit(solution)/shard_map/ppermute | solution.py:62
  118.1 19.5 %all-to-all-start.1 = ((bf16[4,32,2048]{2,1,0:T(8,128)(2,1)}), bf16[4,32,2048]{2,1,0:T(8,128)(2,1)}, u32[]{:S(2)}, u32[]{:S(2)}) async-start(bf16[4,32,2048]{2,1,0:T(8,128)(2,1)} %bitcast.109), calls=%async_computation.1 | async-start | bytes 1048576 | tf_op jit(solution)/shard_map/all_to_all | solution.py:84
  169.1 15.1 %collective-permute-start.26 = (bf16[128,2048]{1,0:T(8,128)(2,1)}, bf16[128,2048]{1,0:T(8,128)(2,1)}, u32[]{:S(2)}, u32[]{:S(2)}) collective-permute-start(bf16[128,2048]{1,0:T(8,128)(2,1)} %slice.285), channel_id=1, source_target_pairs={{0,1},{1,0},{2,3},{3,2},{4,5},{5,4},{6,7},{7,6},{8,9},{9,8},{10,11... | collective-permute-start | bytes 1572872 | tf_op jit(solution)/shard_map/ppermute | solution.py:78
  169.3 19.5 %all-to-all-start.2 = ((bf16[4,32,2048]{2,1,0:T(8,128)(2,1)}), bf16[4,32,2048]{2,1,0:T(8,128)(2,1)}, u32[]{:S(2)}, u32[]{:S(2)}) async-start(bf16[4,32,2048]{2,1,0:T(8,128)(2,1)} %bitcast.108), calls=%async_computation.2 | async-start | bytes 1048576 | tf_op jit(solution)/shard_map/all_to_all | solution.py:84
  173.4 111.1 %reduce-scatter.2.cloned.1.call-start = ((), (), s32[]{:S(2)}) async-start(), calls=%async_computation.6 | async-start | bytes 1310720 | tf_op jit(solution)/shard_map/reduce_scatter | solution.py:257
  221.4 14.0 %collective-permute-start.33 = (bf16[512,512]{1,0:T(8,128)(2,1)S(1)}, bf16[512,512]{1,0:T(8,128)(2,1)S(1)}, u32[]{:S(2)}, u32[]{:S(2)}) collective-permute-start(bf16[512,512]{1,0:T(8,128)(2,1)S(1)} %convolution_convert_fusion.3), channel_id=1, source_target_pairs={{0,2},{2,0},{1,3},{3,1},{4,6},{6,4},{5,7},{7,5},{8,10},{10,8},{9,1... | collective-permute-start | bytes 1572872 | tf_op jit(solution)/shard_map/ppermute | solution.py:237
  222.5 13.7 %collective-permute-start.34 = (bf16[512,512]{1,0:T(8,128)(2,1)S(1)}, bf16[512,512]{1,0:T(8,128)(2,1)S(1)}, u32[]{:S(2)}, u32[]{:S(2)}) collective-permute-start(bf16[512,512]{1,0:T(8,128)(2,1)S(1)} %convolution_convert_fusion.2), channel_id=1, source_target_pairs={{0,4},{4,0},{1,5},{5,1},{2,6},{6,2},{3,7},{7,3},{8,12},{12,8},{9,1... | collective-permute-start | bytes 1572872 | tf_op jit(solution)/shard_map/ppermute | solution.py:238
  236.2 10.5 %collective-permute-start.41 = (f32[258]{0:T(512)S(1)}, f32[258]{0:T(512)S(1)}, u32[]{:S(2)}, u32[]{:S(2)}) collective-permute-start(f32[258]{0:T(512)S(1)} %maximum_add_fusion), channel_id=1, source_target_pairs={{0,8},{8,0},{16,24},{24,16},{1,9},{9,1},{17,25},{25,17},{2,10},{10... | collective-permute-start | bytes 3104 | tf_op jit(solution)/shard_map/ppermute | solution.py:46
  238.9 15.1 %collective-permute-start.37 = (bf16[512,512]{1,0:T(8,128)(2,1)}, bf16[512,512]{1,0:T(8,128)(2,1)S(1)}, u32[]{:S(2)}, u32[]{:S(2)}) collective-permute-start(bf16[512,512]{1,0:T(8,128)(2,1)} %convolution_convert_fusion.1), channel_id=1, source_target_pairs={{0,2},{2,0},{1,3},{3,1},{4,6},{6,4},{5,7},{7,5},{8,10},{10,8},{9,1... | collective-permute-start | bytes 1572872 | tf_op jit(solution)/shard_map/ppermute | solution.py:250
  240.4 15.2 %collective-permute-start.38 = (bf16[512,512]{1,0:T(8,128)(2,1)}, bf16[512,512]{1,0:T(8,128)(2,1)}, u32[]{:S(2)}, u32[]{:S(2)}) collective-permute-start(bf16[512,512]{1,0:T(8,128)(2,1)} %fusion.28), channel_id=1, source_target_pairs={{0,4},{4,0},{1,5},{5,1},{2,6},{6,2},{3,7},{7,3},{8,12},{12,8},{9,1... | collective-permute-start | bytes 1572872 | tf_op jit(solution)/shard_map/ppermute | solution.py:255
  243.8 19.0 %collective-permute-start.39 = (bf16[512,512]{1,0:T(8,128)(2,1)}, bf16[512,512]{1,0:T(8,128)(2,1)S(1)}, u32[]{:S(2)}, u32[]{:S(2)}) collective-permute-start(bf16[512,512]{1,0:T(8,128)(2,1)} %fusion.29), channel_id=1, source_target_pairs={{0,2},{2,0},{1,3},{3,1},{4,6},{6,4},{5,7},{7,5},{8,10},{10,8},{9,1... | collective-permute-start | bytes 1572872 | tf_op jit(solution)/shard_map/ppermute | solution.py:254
  245.0 19.5 %collective-permute-start.40 = (bf16[512,512]{1,0:T(8,128)(2,1)}, bf16[512,512]{1,0:T(8,128)(2,1)}, u32[]{:S(2)}, u32[]{:S(2)}) collective-permute-start(bf16[512,512]{1,0:T(8,128)(2,1)} %convolution_convert_fusion), channel_id=1, source_target_pairs={{0,4},{4,0},{1,5},{5,1},{2,6},{6,2},{3,7},{7,3},{8,12},{12,8},{9,1... | collective-permute-start | bytes 1572872 | tf_op jit(solution)/shard_map/ppermute | solution.py:251
  267.2 20.0 %collective-permute-start.45 = (bf16[256,256]{1,0:T(8,128)(2,1)S(1)}, bf16[256,256]{1,0:T(8,128)(2,1)S(1)}, u32[]{:S(2)}, u32[]{:S(2)}) collective-permute-start(bf16[256,256]{1,0:T(8,128)(2,1)S(1)} %get-tuple-element.157), channel_id=1, source_target_pairs={{0,2},{2,0},{1,3},{3,1},{4,6},{6,4},{5,7},{7,5},{8,10},{10,8},{9,1... | collective-permute-start | bytes 393224 | tf_op jit(solution)/shard_map/ppermute | solution.py:70
  268.7 18.6 %collective-permute-start.46 = (bf16[256,256]{1,0:T(8,128)(2,1)S(1)}, bf16[256,256]{1,0:T(8,128)(2,1)S(1)}, u32[]{:S(2)}, u32[]{:S(2)}) collective-permute-start(bf16[256,256]{1,0:T(8,128)(2,1)S(1)} %get-tuple-element.156), channel_id=1, source_target_pairs={{0,4},{4,0},{1,5},{5,1},{2,6},{6,2},{3,7},{7,3},{8,12},{12,8},{9,1... | collective-permute-start | bytes 393224 | tf_op jit(solution)/shard_map/ppermute | solution.py:71
  269.0 18.2 %collective-permute-start.47 = (bf16[256,256]{1,0:T(8,128)(2,1)S(1)}, bf16[256,256]{1,0:T(8,128)(2,1)S(1)}, u32[]{:S(2)}, u32[]{:S(2)}) collective-permute-start(bf16[256,256]{1,0:T(8,128)(2,1)S(1)} %get-tuple-element.155), channel_id=1, source_target_pairs={{0,6},{2,4},{4,2},{6,0},{1,7},{3,5},{5,3},{7,1},{8,14},{10,12},{12... | collective-permute-start | bytes 393224 | tf_op jit(solution)/shard_map/ppermute | solution.py:72
  272.4 26.2 %all-to-all-start.3 = ((bf16[4,256,512]{2,1,0:T(8,128)(2,1)}), bf16[4,256,512]{2,1,0:T(8,128)(2,1)S(1)}, u32[]{:S(2)}, u32[]{:S(2)}) async-start(bf16[4,256,512]{2,1,0:T(8,128)(2,1)} %bitcast.38), calls=%async_computation.4 | async-start | bytes 2097152 | tf_op jit(solution)/shard_map/all_to_all | solution.py:268
  276.3 27.5 %all-gather.7.cloned.1.call-start = ((), (), s32[]{:S(2)}) async-start(), calls=%async_computation.7 | async-start | bytes 1310720 | tf_op jit(solution)/shard_map/all_gather | solution.py:259
  (71 other events, 406.3 us)
Sparse Core Ops, SparseCore 0:
  63.0 25.1 all-gather.8
  118.3 50.5 all-gather.4
  250.4 24.8 reduce-scatter.1
  287.4 16.3 all-gather.6

commit v3 on v2

--- a/solution.py
+++ b/solution.py
@@ -266,6 +266,10 @@
     else:
         block, tail, g_late = tied((block, tail, g_late))
     grad_one = lax.all_to_all(block, "z", 0, 1, tiled=True).astype(F32)
+    terms = lax.dynamic_index_in_dim(tail[:n].reshape(2, planes, quarter), at_z, 1, keepdims=False)
+    terms = in_order(terms[0], terms[1], core)
+    tail = jnp.concatenate([tail[n:], terms])
+    tail_x, g_late = tied((lax.ppermute(tail, "x", SWAP), g_late))
 
     if factors:
         own_act, x_act, y_act, d_act = act_units
@@ -297,10 +301,6 @@
     output = ends[0]
     grad_tokens = cotangent.astype(F32) + ends[1].astype(F32)
 
-    terms = lax.dynamic_index_in_dim(tail[:n].reshape(2, planes, quarter), at_z, 1, keepdims=False)
-    terms = in_order(terms[0], terms[1], core)
-    tail = jnp.concatenate([tail[n:], terms])
-    tail_x = lax.ppermute(tail, "x", SWAP)
     logdet = in_order(tail[2:], tail_x[2:], at_x)
     inner = sum_over(tail[:2] + tail_x[:2], ("y",))
 

time: 315 us -> 315 us (level)
  transfers between devices with their start and end apart: 56 -> 56, of which waited for: 25 -> 25; matrix products, arithmetic and copies ran while one was open for 29% -> 28% of each run, Pallas kernels for 0% -> 0%
where the time goes in v3:
time: 315 us; the launch traced here: 313 us
  waiting for transfers between devices  85.3 us (27%)
  starting transfers between devices  59.2 us (19%)
  other arithmetic  52 us (17%)
  matrix products  35 us (11%)
  local copies, waits for them, and re-layouts  32.4 us (10%)
  blocking collectives  32.2 us (10%)
  between operations  17.4 us (6%)
    all_gather x2, blocking collectives, gather_rows(): return with_other_core(lax.all_gather(quarter, 'z', axis=0, tiled=True))  32.2 us
    ppermute x2, waiting for transfers between devices, spread(): x_low = lax.ppermute(block[half:], 'x', SWAP)  18.4 us
    dot_general x10, matrix products, contract_rows(): lax.dot_general(left, right, (((0,), (0,)), ((), ())), preferred_element_...  15.3 us
    ppermute x12, starting transfers between devices, sum_over(): values = values + lax.ppermute(values, name, pairs)  13.8 us
    unnamed x102, local copies, waits for them, and re-layouts  13.8 us
    dot_general x8, matrix products, times(): return jnp.dot(left, right, preferred_element_type=F32)  11.8 us
    ppermute x12, waiting for transfers between devices, sum_over(): values = values + lax.ppermute(values, name, pairs)  10.7 us
    ppermute x1, waiting for transfers between devices, on_device(): across_x = lax.ppermute(across_x, 'x', SWAP)  9.97 us
  transfers between devices with their start and end apart: 56, of which 25 were waited for; matrix products, arithmetic and copies ran while one was open for 28% of the time, Pallas kernels for 0%

profile of v3, /device:TPU:0, one launch (start us, length us, event | category | flops | bytes accessed | tf_op | source)
XLA Modules:
  0.0 313.4 jit_solution(9679280893084430072)
XLA Ops:
  7.2 2.4 fusion.86
  9.6 2.9 collective-permute-start.6
  22.1 2.6 collective-permute-start.3
  27.1 3.0 collective-permute-done.1
  31.4 3.5 %all-to-all-start = ((bf16[256,4,512]{0,2,1:T(8,128)(2,1)}), bf16[256,4,512]{0,2,1:T(8,128)(2,1)S(1)}, u32[]{:S(2)}, u32[]{:S(2)}) async-start(bf16[256,4,512]{0,2,1:T(8,128)(2,1)} %bitcast.3), calls=%async_computation | async-start | bytes 2097152 | tf_op jit(solution)/shard_map/all_to_all | solution.py:137
  35.0 2.4 collective-permute-done.7
  47.1 6.2 %collective-permute-done.21 = bf16[128,2048]{1,0:T(8,128)(2,1)S(1)} collective-permute-done((bf16[128,2048]{1,0:T(8,128)(2,1)S(1)}, bf16[128,2048]{1,0:T(8,128)(2,1)S(1)}, u32[]{:S(2)}, u32[]{:S(2)}) %collective-permute-start.21) | collective-permute-done | bytes 524320 | tf_op jit(solution)/shard_map/ppermute | solution.py:61
  53.9 4.0 %all-to-all-done = bf16[256,4,512]{0,2,1:T(8,128)(2,1)S(1)} async-done(((bf16[256,4,512]{0,2,1:T(8,128)(2,1)}), bf16[256,4,512]{0,2,1:T(8,128)(2,1)S(1)}, u32[]{:S(2)}, u32[]{:S(2)}) %all-to-all-start) | async-done | bytes 1048608 | tf_op jit(solution)/shard_map/all_to_all | solution.py:137
  62.9 2.7 broadcast_select_fusion.1
  66.2 18.4 %collective-permute-done.4 = bf16[512,512]{1,0:T(8,128)(2,1)} collective-permute-done((bf16[512,512]{1,0:T(8,128)(2,1)}, bf16[512,512]{1,0:T(8,128)(2,1)}, u32[]{:S(2)}, u32[]{:S(2)}) %collective-permute-start.4) | collective-permute-done | bytes 524320 | tf_op jit(solution)/shard_map/ppermute | solution.py:56
  106.2 2.3 pad_maximum_fusion.8
  111.3 2.3 fusion.18
  118.1 4.2 %all-to-all-start.1 = ((bf16[4,32,2048]{2,1,0:T(8,128)(2,1)}), bf16[4,32,2048]{2,1,0:T(8,128)(2,1)}, u32[]{:S(2)}, u32[]{:S(2)}) async-start(bf16[4,32,2048]{2,1,0:T(8,128)(2,1)} %bitcast.109), calls=%async_computation.1 | async-start | bytes 1048576 | tf_op jit(solution)/shard_map/all_to_all | solution.py:84
  122.3 6.4 %fusion.20 = f32[512,1024]{1,0:T(8,128)S(1)} fusion(bf16[256,2048]{1,0:T(8,128)(2,1)} %pad_maximum_fusion.8, bf16[256,2048]{1,0:T(8,128)(2,1)} %fusion.17, bf16[256,2048]{1,0:T(8,128)(2,1)} %get-tuple-element.143, bf16[256,2048]{1,0:T(8,128)(2,1)} %get-tuple-element.142, bf16[256,2048]{1,0:T(8,128)(2,1)} %get-tuple-element.141, ...), kind=kOutput, calls=%fused_computation.49 | convolution fusion | flops 2168455168 | bytes 8388608 | tf_op jit(solution)/shard_map/dot_general | solution.py:32
  131.4 6.3 %all-to-all-done.1 = bf16[4,32,2048]{2,1,0:T(8,128)(2,1)} async-done(((bf16[4,32,2048]{2,1,0:T(8,128)(2,1)}), bf16[4,32,2048]{2,1,0:T(8,128)(2,1)}, u32[]{:S(2)}, u32[]{:S(2)}) %all-to-all-start.1) | async-done | bytes 524320 | tf_op jit(solution)/shard_map/all_to_all | solution.py:84
  138.8 15.9 %all_gather.20 = bf16[128,2048]{1,0:T(8,128)(2,1)S(1)} all-gather(bf16[32,2048]{1,0:T(8,128)(2,1)S(1)} %reduce_sum.91), channel_id=1, replica_groups=mesh['z'=4,'y'=2,'x'=2,'c'=2] {'z'}, dimensions={0}, use_global_device_ids=true | all-gather | bytes 655360 | tf_op jit(solution)/shard_map/all_gather | solution.py:93
  157.6 3.0 convolution_multiply_fusion.5
  169.3 4.1 %all-to-all-start.2 = ((bf16[4,32,2048]{2,1,0:T(8,128)(2,1)}), bf16[4,32,2048]{2,1,0:T(8,128)(2,1)}, u32[]{:S(2)}, u32[]{:S(2)}) async-start(bf16[4,32,2048]{2,1,0:T(8,128)(2,1)} %bitcast.108), calls=%async_computation.2 | async-start | bytes 1048576 | tf_op jit(solution)/shard_map/all_to_all | solution.py:84
  174.3 2.9 collective-permute-done.27
  181.8 2.4 collective-permute-start.31
  186.5 2.3 all-to-all-done.2
  190.0 16.4 %all_gather.22 = bf16[128,2048]{1,0:T(8,128)(2,1)} all-gather(bf16[32,2048]{1,0:T(8,128)(2,1)S(1)} %reduce_sum.92), channel_id=1, replica_groups=mesh['z'=4,'y'=2,'x'=2,'c'=2] {'z'}, dimensions={0}, use_global_device_ids=true | all-gather | bytes 655360 | tf_op jit(solution)/shard_map/all_gather | solution.py:93
  225.4 10.0 %collective-permute-done.33 = bf16[512,512]{1,0:T(8,128)(2,1)S(1)} collective-permute-done((bf16[512,512]{1,0:T(8,128)(2,1)S(1)}, bf16[512,512]{1,0:T(8,128)(2,1)S(1)}, u32[]{:S(2)}, u32[]{:S(2)}) %collective-permute-start.33) | collective-permute-done | bytes 524320 | tf_op jit(solution)/shard_map/ppermute | solution.py:237
  246.0 2.5 collective-permute-start.42
  250.5 2.5 collective-permute-done.37
  256.4 5.5 %collective-permute-done.39 = bf16[512,512]{1,0:T(8,128)(2,1)S(1)} collective-permute-done((bf16[512,512]{1,0:T(8,128)(2,1)}, bf16[512,512]{1,0:T(8,128)(2,1)S(1)}, u32[]{:S(2)}, u32[]{:S(2)}) %collective-permute-start.39) | collective-permute-done | bytes 524320 | tf_op jit(solution)/shard_map/ppermute | solution.py:254
  268.0 3.9 %all-to-all-start.3 = ((bf16[4,256,512]{2,1,0:T(8,128)(2,1)}), bf16[4,256,512]{2,1,0:T(8,128)(2,1)S(1)}, u32[]{:S(2)}, u32[]{:S(2)}) async-start(bf16[4,256,512]{2,1,0:T(8,128)(2,1)} %bitcast.38), calls=%async_computation.4 | async-start | bytes 2097152 | tf_op jit(solution)/shard_map/all_to_all | solution.py:268
  278.6 2.6 collective-permute-done.44
  286.6 3.8 %fusion.7 = f32[256,2048]{1,0:T(8,128)S(1)} fusion(s32[2048]{0:T(1024)S(1)} %iota_multiply_fusion, s32[1024]{0:T(1024)S(1)} %add_multiply_fusion, bf16[256,256]{1,0:T(8,128)(2,1)S(1)} %collective-permute-done.47, bf16[256,256]{1,0:T(8,128)(2,1)S(1)} %collective-permute-done.46, bf16[256,256]{1,0:T(8,128)(2,1)S(1)} %collective-permute-done.45, ...), kind=kOutput, calls=%fused_computation.20 | convolution fusion | flops 1101004800 | bytes 2633728 | tf_op jit(solution)/shard_map/dot_general | solution.py:28
  290.4 3.3 %fusion.10 = f32[256,2048]{1,0:T(8,128)} fusion(f32[256,2048]{1,0:T(8,128)S(1)} %fusion.7, bf16[1024,2048]{1,0:T(8,128)(2,1)S(1)} %copy-done.45, f32[]{:T(128)} %get-tuple-element.173, f32[2048]{0:T(1024)S(1)} %copy-done.41, f32[256]{0:T(256)S(1)} %convert_multiply_fusion, f32[]{:T(128)S(6)} %mul.281, bf16[512,256]{1,0:T(8,128)(2,1)S(1)} %get-tuple-element.157, ...), kind=kOutput, calls=%fused_computation.37 | convolution fusion | flops 1077411840 | bytes 8922120 | tf_op jit(solution)/shard_map/dot_general | solution.py:28
  296.7 2.4 subtract_multiply_fusion
  299.1 4.7 %all-gather.7.cloned.1.call-done = bf16[2,128,2048]{2,1,0:T(8,128)(2,1)} async-done(((bf16[2,32,2048]{2,1,0:T(8,128)(2,1)}), bf16[2,128,2048]{2,1,0:T(8,128)(2,1)}) %all-gather.7.cloned.1.call-update) | async-done | bytes 1048592 | tf_op jit(solution)/shard_map/all_gather | solution.py:259
  (319 shorter events, 138.3 us)
Async XLA Ops:
  9.6 25.4 %collective-permute-start.6 = (bf16[128,2048]{1,0:T(8,128)(2,1)}, bf16[128,2048]{1,0:T(8,128)(2,1)}, u32[]{:S(2)}, u32[]{:S(2)}) collective-permute-start(bf16[128,2048]{1,0:T(8,128)(2,1)} %get-tuple-element.153), channel_id=1, source_target_pairs={{0,2},{2,0},{1,3},{3,1},{4,6},{6,4},{5,7},{7,5},{8,10},{10,8},{9,1... | collective-permute-start | bytes 1572872 | tf_op jit(solution)/shard_map/ppermute | solution.py:56
  12.6 26.9 %collective-permute-start.19 = (bf16[128,2048]{1,0:T(8,128)(2,1)}, bf16[128,2048]{1,0:T(8,128)(2,1)S(1)}, u32[]{:S(2)}, u32[]{:S(2)}) collective-permute-start(bf16[128,2048]{1,0:T(8,128)(2,1)} %get-tuple-element.153), channel_id=1, source_target_pairs={{0,4},{4,0},{1,5},{5,1},{2,6},{6,2},{3,7},{7,3},{8,12},{12,8},{9,1... | collective-permute-start | bytes 1572872 | tf_op jit(solution)/shard_map/ppermute | solution.py:59
  19.0 18.3 %collective-permute-start.7 = (bf16[128,2048]{1,0:T(8,128)(2,1)}, bf16[128,2048]{1,0:T(8,128)(2,1)S(1)}, u32[]{:S(2)}, u32[]{:S(2)}) collective-permute-start(bf16[128,2048]{1,0:T(8,128)(2,1)} %get-tuple-element.152), channel_id=1, source_target_pairs={{0,4},{4,0},{1,5},{5,1},{2,6},{6,2},{3,7},{7,3},{8,12},{12,8},{9,1... | collective-permute-start | bytes 1572872 | tf_op jit(solution)/shard_map/ppermute | solution.py:57
  26.6 14.9 %collective-permute-start.20 = (bf16[128,2048]{1,0:T(8,128)(2,1)}, bf16[128,2048]{1,0:T(8,128)(2,1)}, u32[]{:S(2)}, u32[]{:S(2)}) collective-permute-start(bf16[128,2048]{1,0:T(8,128)(2,1)} %get-tuple-element.152), channel_id=1, source_target_pairs={{0,2},{2,0},{1,3},{3,1},{4,6},{6,4},{5,7},{7,5},{8,10},{10,8},{9,1... | collective-permute-start | bytes 1572872 | tf_op jit(solution)/shard_map/ppermute | solution.py:58
  31.4 26.5 %all-to-all-start = ((bf16[256,4,512]{0,2,1:T(8,128)(2,1)}), bf16[256,4,512]{0,2,1:T(8,128)(2,1)S(1)}, u32[]{:S(2)}, u32[]{:S(2)}) async-start(bf16[256,4,512]{0,2,1:T(8,128)(2,1)} %bitcast.3), calls=%async_computation | async-start | bytes 2097152 | tf_op jit(solution)/shard_map/all_to_all | solution.py:137
  35.0 60.2 %all-gather.9.cloned.1.call-start = ((), (), s32[]{:S(2)}) async-start(), calls=%async_computation.8 | async-start | bytes 1310720 | tf_op jit(solution)/shard_map/all_gather | solution.py:161
  37.4 9.7 %collective-permute-start.8 = (f32[4097]{0:T(1024)S(1)}, f32[4097]{0:T(1024)S(1)}, u32[]{:S(2)}, u32[]{:S(2)}) collective-permute-start(f32[4097]{0:T(1024)S(1)} %add.232), channel_id=1, source_target_pairs={{0,4},{4,0},{1,5},{5,1},{2,6},{6,2},{3,7},{7,3},{8,12},{12,8},{9,1... | collective-permute-start | bytes 49172 | tf_op jit(solution)/shard_map/ppermute | solution.py:46
  38.9 14.3 %collective-permute-start.21 = (bf16[128,2048]{1,0:T(8,128)(2,1)S(1)}, bf16[128,2048]{1,0:T(8,128)(2,1)S(1)}, u32[]{:S(2)}, u32[]{:S(2)}) collective-permute-start(bf16[128,2048]{1,0:T(8,128)(2,1)S(1)} %collective-permute-done.7), channel_id=1, source_target_pairs={{0,2},{2,0},{1,3},{3,1},{4,6},{6,4},{5,7},{7,5},{8,10},{10,8},{9,1... | collective-permute-start | bytes 1572872 | tf_op jit(solution)/shard_map/ppermute | solution.py:61
  39.5 14.3 %collective-permute-start.22 = (bf16[128,2048]{1,0:T(8,128)(2,1)}, bf16[128,2048]{1,0:T(8,128)(2,1)S(1)}, u32[]{:S(2)}, u32[]{:S(2)}) collective-permute-start(bf16[128,2048]{1,0:T(8,128)(2,1)} %collective-permute-done.6), channel_id=1, source_target_pairs={{0,4},{4,0},{1,5},{5,1},{2,6},{6,2},{3,7},{7,3},{8,12},{12,8},{9,1... | collective-permute-start | bytes 1572872 | tf_op jit(solution)/shard_map/ppermute | solution.py:62
  59.3 25.3 %collective-permute-start.5 = (bf16[512,512]{1,0:T(8,128)(2,1)S(1)}, bf16[512,512]{1,0:T(8,128)(2,1)}, u32[]{:S(2)}, u32[]{:S(2)}) collective-permute-start(bf16[512,512]{1,0:T(8,128)(2,1)S(1)} %get-tuple-element.154), channel_id=1, source_target_pairs={{0,4},{4,0},{1,5},{5,1},{2,6},{6,2},{3,7},{7,3},{8,12},{12,8},{9,1... | collective-permute-start | bytes 1572872 | tf_op jit(solution)/shard_map/ppermute | solution.py:57
  60.8 27.7 %collective-permute-start.17 = (bf16[512,512]{1,0:T(8,128)(2,1)S(1)}, bf16[512,512]{1,0:T(8,128)(2,1)}, u32[]{:S(2)}, u32[]{:S(2)}) collective-permute-start(bf16[512,512]{1,0:T(8,128)(2,1)S(1)} %get-tuple-element.154), channel_id=1, source_target_pairs={{0,2},{2,0},{1,3},{3,1},{4,6},{6,4},{5,7},{7,5},{8,10},{10,8},{9,1... | collective-permute-start | bytes 1572872 | tf_op jit(solution)/shard_map/ppermute | solution.py:58
  61.3 23.2 %collective-permute-start.4 = (bf16[512,512]{1,0:T(8,128)(2,1)}, bf16[512,512]{1,0:T(8,128)(2,1)}, u32[]{:S(2)}, u32[]{:S(2)}) collective-permute-start(bf16[512,512]{1,0:T(8,128)(2,1)} %get-tuple-element.155), channel_id=1, source_target_pairs={{0,2},{2,0},{1,3},{3,1},{4,6},{6,4},{5,7},{7,5},{8,10},{10,8},{9,1... | collective-permute-start | bytes 1572872 | tf_op jit(solution)/shard_map/ppermute | solution.py:56
  62.8 127.1 %all-gather.5.cloned.1.call-start = ((), (), s32[]{:S(2)}) async-start(), calls=%async_computation.5 | async-start | bytes 5242880 | tf_op jit(solution)/shard_map/all_gather | solution.py:188
  65.6 23.9 %collective-permute-start.16 = (bf16[512,512]{1,0:T(8,128)(2,1)}, bf16[512,512]{1,0:T(8,128)(2,1)S(1)}, u32[]{:S(2)}, u32[]{:S(2)}) collective-permute-start(bf16[512,512]{1,0:T(8,128)(2,1)} %get-tuple-element.155), channel_id=1, source_target_pairs={{0,4},{4,0},{1,5},{5,1},{2,6},{6,2},{3,7},{7,3},{8,12},{12,8},{9,1... | collective-permute-start | bytes 1572872 | tf_op jit(solution)/shard_map/ppermute | solution.py:59
  84.6 18.3 %collective-permute-start.11 = (bf16[512,512]{1,0:T(8,128)(2,1)}, bf16[512,512]{1,0:T(8,128)(2,1)S(1)}, u32[]{:S(2)}, u32[]{:S(2)}) collective-permute-start(bf16[512,512]{1,0:T(8,128)(2,1)} %collective-permute-done.5), channel_id=1, source_target_pairs={{0,2},{2,0},{1,3},{3,1},{4,6},{6,4},{5,7},{7,5},{8,10},{10,8},{9,1... | collective-permute-start | bytes 1572872 | tf_op jit(solution)/shard_map/ppermute | solution.py:61
  85.1 18.5 %collective-permute-start.12 = (bf16[512,512]{1,0:T(8,128)(2,1)}, bf16[512,512]{1,0:T(8,128)(2,1)}, u32[]{:S(2)}, u32[]{:S(2)}) collective-permute-start(bf16[512,512]{1,0:T(8,128)(2,1)} %collective-permute-done.4), channel_id=1, source_target_pairs={{0,4},{4,0},{1,5},{5,1},{2,6},{6,2},{3,7},{7,3},{8,12},{12,8},{9,1... | collective-permute-start | bytes 1572872 | tf_op jit(solution)/shard_map/ppermute | solution.py:62
  118.1 19.5 %all-to-all-start.1 = ((bf16[4,32,2048]{2,1,0:T(8,128)(2,1)}), bf16[4,32,2048]{2,1,0:T(8,128)(2,1)}, u32[]{:S(2)}, u32[]{:S(2)}) async-start(bf16[4,32,2048]{2,1,0:T(8,128)(2,1)} %bitcast.109), calls=%async_computation.1 | async-start | bytes 1048576 | tf_op jit(solution)/shard_map/all_to_all | solution.py:84
  169.1 15.1 %collective-permute-start.26 = (bf16[128,2048]{1,0:T(8,128)(2,1)}, bf16[128,2048]{1,0:T(8,128)(2,1)}, u32[]{:S(2)}, u32[]{:S(2)}) collective-permute-start(bf16[128,2048]{1,0:T(8,128)(2,1)} %slice.285), channel_id=1, source_target_pairs={{0,1},{1,0},{2,3},{3,2},{4,5},{5,4},{6,7},{7,6},{8,9},{9,8},{10,11... | collective-permute-start | bytes 1572872 | tf_op jit(solution)/shard_map/ppermute | solution.py:78
  169.3 19.5 %all-to-all-start.2 = ((bf16[4,32,2048]{2,1,0:T(8,128)(2,1)}), bf16[4,32,2048]{2,1,0:T(8,128)(2,1)}, u32[]{:S(2)}, u32[]{:S(2)}) async-start(bf16[4,32,2048]{2,1,0:T(8,128)(2,1)} %bitcast.108), calls=%async_computation.2 | async-start | bytes 1048576 | tf_op jit(solution)/shard_map/all_to_all | solution.py:84
  173.4 110.5 %reduce-scatter.2.cloned.1.call-start = ((), (), s32[]{:S(2)}) async-start(), calls=%async_computation.6 | async-start | bytes 1310720 | tf_op jit(solution)/shard_map/reduce_scatter | solution.py:257
  221.4 14.0 %collective-permute-start.33 = (bf16[512,512]{1,0:T(8,128)(2,1)S(1)}, bf16[512,512]{1,0:T(8,128)(2,1)S(1)}, u32[]{:S(2)}, u32[]{:S(2)}) collective-permute-start(bf16[512,512]{1,0:T(8,128)(2,1)S(1)} %convolution_convert_fusion.3), channel_id=1, source_target_pairs={{0,2},{2,0},{1,3},{3,1},{4,6},{6,4},{5,7},{7,5},{8,10},{10,8},{9,1... | collective-permute-start | bytes 1572872 | tf_op jit(solution)/shard_map/ppermute | solution.py:237
  222.5 13.7 %collective-permute-start.34 = (bf16[512,512]{1,0:T(8,128)(2,1)S(1)}, bf16[512,512]{1,0:T(8,128)(2,1)S(1)}, u32[]{:S(2)}, u32[]{:S(2)}) collective-permute-start(bf16[512,512]{1,0:T(8,128)(2,1)S(1)} %convolution_convert_fusion.2), channel_id=1, source_target_pairs={{0,4},{4,0},{1,5},{5,1},{2,6},{6,2},{3,7},{7,3},{8,12},{12,8},{9,1... | collective-permute-start | bytes 1572872 | tf_op jit(solution)/shard_map/ppermute | solution.py:238
  236.2 9.8 %collective-permute-start.41 = (f32[258]{0:T(512)S(1)}, f32[258]{0:T(512)S(1)}, u32[]{:S(2)}, u32[]{:S(2)}) collective-permute-start(f32[258]{0:T(512)S(1)} %maximum_add_fusion), channel_id=1, source_target_pairs={{0,8},{8,0},{16,24},{24,16},{1,9},{9,1},{17,25},{25,17},{2,10},{10... | collective-permute-start | bytes 3104 | tf_op jit(solution)/shard_map/ppermute | solution.py:46
  238.1 14.9 %collective-permute-start.37 = (bf16[512,512]{1,0:T(8,128)(2,1)S(1)}, bf16[512,512]{1,0:T(8,128)(2,1)S(1)}, u32[]{:S(2)}, u32[]{:S(2)}) collective-permute-start(bf16[512,512]{1,0:T(8,128)(2,1)S(1)} %convolution_convert_fusion.1), channel_id=1, source_target_pairs={{0,2},{2,0},{1,3},{3,1},{4,6},{6,4},{5,7},{7,5},{8,10},{10,8},{9,1... | collective-permute-start | bytes 1572872 | tf_op jit(solution)/shard_map/ppermute | solution.py:250
  239.7 15.2 %collective-permute-start.38 = (bf16[512,512]{1,0:T(8,128)(2,1)}, bf16[512,512]{1,0:T(8,128)(2,1)}, u32[]{:S(2)}, u32[]{:S(2)}) collective-permute-start(bf16[512,512]{1,0:T(8,128)(2,1)} %fusion.28), channel_id=1, source_target_pairs={{0,4},{4,0},{1,5},{5,1},{2,6},{6,2},{3,7},{7,3},{8,12},{12,8},{9,1... | collective-permute-start | bytes 1572872 | tf_op jit(solution)/shard_map/ppermute | solution.py:255
  243.1 18.8 %collective-permute-start.39 = (bf16[512,512]{1,0:T(8,128)(2,1)}, bf16[512,512]{1,0:T(8,128)(2,1)S(1)}, u32[]{:S(2)}, u32[]{:S(2)}) collective-permute-start(bf16[512,512]{1,0:T(8,128)(2,1)} %fusion.29), channel_id=1, source_target_pairs={{0,2},{2,0},{1,3},{3,1},{4,6},{6,4},{5,7},{7,5},{8,10},{10,8},{9,1... | collective-permute-start | bytes 1572872 | tf_op jit(solution)/shard_map/ppermute | solution.py:254
  244.3 19.5 %collective-permute-start.40 = (bf16[512,512]{1,0:T(8,128)(2,1)}, bf16[512,512]{1,0:T(8,128)(2,1)}, u32[]{:S(2)}, u32[]{:S(2)}) collective-permute-start(bf16[512,512]{1,0:T(8,128)(2,1)} %convolution_convert_fusion), channel_id=1, source_target_pairs={{0,4},{4,0},{1,5},{5,1},{2,6},{6,2},{3,7},{7,3},{8,12},{12,8},{9,1... | collective-permute-start | bytes 1572872 | tf_op jit(solution)/shard_map/ppermute | solution.py:251
  268.0 27.7 %all-to-all-start.3 = ((bf16[4,256,512]{2,1,0:T(8,128)(2,1)}), bf16[4,256,512]{2,1,0:T(8,128)(2,1)S(1)}, u32[]{:S(2)}, u32[]{:S(2)}) async-start(bf16[4,256,512]{2,1,0:T(8,128)(2,1)} %bitcast.38), calls=%async_computation.4 | async-start | bytes 2097152 | tf_op jit(solution)/shard_map/all_to_all | solution.py:268
  271.9 31.9 %all-gather.7.cloned.1.call-start = ((), (), s32[]{:S(2)}) async-start(), calls=%async_computation.7 | async-start | bytes 1310720 | tf_op jit(solution)/shard_map/all_gather | solution.py:259
  274.1 12.5 %collective-permute-start.45 = (bf16[256,256]{1,0:T(8,128)(2,1)S(1)}, bf16[256,256]{1,0:T(8,128)(2,1)S(1)}, u32[]{:S(2)}, u32[]{:S(2)}) collective-permute-start(bf16[256,256]{1,0:T(8,128)(2,1)S(1)} %get-tuple-element.161), channel_id=1, source_target_pairs={{0,2},{2,0},{1,3},{3,1},{4,6},{6,4},{5,7},{7,5},{8,10},{10,8},{9,1... | collective-permute-start | bytes 393224 | tf_op jit(solution)/shard_map/ppermute | solution.py:70
  274.7 11.9 %collective-permute-start.46 = (bf16[256,256]{1,0:T(8,128)(2,1)S(1)}, bf16[256,256]{1,0:T(8,128)(2,1)S(1)}, u32[]{:S(2)}, u32[]{:S(2)}) collective-permute-start(bf16[256,256]{1,0:T(8,128)(2,1)S(1)} %get-tuple-element.160), channel_id=1, source_target_pairs={{0,4},{4,0},{1,5},{5,1},{2,6},{6,2},{3,7},{7,3},{8,12},{12,8},{9,1... | collective-permute-start | bytes 393224 | tf_op jit(solution)/shard_map/ppermute | solution.py:71
  275.6 11.0 %collective-permute-start.47 = (bf16[256,256]{1,0:T(8,128)(2,1)S(1)}, bf16[256,256]{1,0:T(8,128)(2,1)S(1)}, u32[]{:S(2)}, u32[]{:S(2)}) collective-permute-start(bf16[256,256]{1,0:T(8,128)(2,1)S(1)} %get-tuple-element.159), channel_id=1, source_target_pairs={{0,6},{2,4},{4,2},{6,0},{1,7},{3,5},{5,3},{7,1},{8,14},{10,12},{12... | collective-permute-start | bytes 393224 | tf_op jit(solution)/shard_map/ppermute | solution.py:72
  (71 other events, 404.3 us)
Sparse Core Ops, SparseCore 0:
  63.0 25.1 all-gather.8
  118.3 50.5 all-gather.4
  249.7 24.8 reduce-scatter.1
  286.7 17.0 all-gather.6
